TPU v7x, 32 devices: a whole 2x2x4 slice. The times are simulated.
32 devices in a mesh: pop: 2 (over y), hid: 8 (over z, x), tok: 2 (over core).
Axes of the slice: x: 2, y: 2, z: 4, core: 2. Of those that a mesh axis runs over, the one named last changes fastest.
Arguments:
- tokens: bfloat16 [3072, 8192], P(('pop', 'tok'), 'hid'), parts along dimension 0, may hold values from -6 to 6
- teacher: bfloat16 [3072, 8192], P(('pop', 'tok'), 'hid'), parts along dimension 0, may hold values from -8 to 8
- assigned: int32 [3072], P(('pop', 'tok')), parts along dimension 0, may hold values 0 or 1
- bfly_in: bfloat16 [256, 8, 64, 256], P(('pop', 'hid')), parts along dimension 0, may hold values from -0.25 to 0.25
- bfly_out: bfloat16 [256, 8, 256, 64], P(('pop', 'hid')), parts along dimension 0, may hold values from -0.125 to 0.125
- low_in_a: bfloat16 [16384, 512], P(('pop', 'hid')), parts along dimension 0, may hold values from -0.0625 to 0.0625
- low_in_b: bfloat16 [1024, 32768], P('pop', 'hid'), parts along dimension 0, may hold values from -0.25 to 0.25
- low_out_a: bfloat16 [65536, 512], P(('pop', 'hid')), parts along dimension 0, may hold values from -0.03125 to 0.03125
- low_out_b: bfloat16 [1024, 8192], P('pop', 'hid'), parts along dimension 0, may hold values from -0.25 to 0.25
- hidden_order: int32 [128, 256], P('hid'), may hold values from 0 to 255, each once within a row
Outputs:
- student: bfloat16 [3072, 8192], P(('pop', 'tok'), 'hid'), parts along dimension 0
- grad_tokens: bfloat16 [3072, 8192], P(('pop', 'tok'), 'hid'), parts along dimension 0
- grad_bfly_in: float32 [256, 8, 64, 256], P(('pop', 'hid'), None, None, 'tok'), parts along dimension 0
- grad_bfly_out: float32 [256, 8, 256, 64], P(('pop', 'hid'), None, 'tok'), parts along dimension 0
- grad_low_in_a: float32 [16384, 512], P(('pop', 'hid'), 'tok'), parts along dimension 0
- grad_low_in_b: float32 [1024, 32768], P(('pop', 'tok'), 'hid'), parts along dimension 0
- grad_low_out_a: float32 [65536, 512], P(('pop', 'hid'), 'tok'), parts along dimension 0
- grad_low_out_b: float32 [1024, 8192], P(('pop', 'tok'), 'hid'), parts along dimension 0
There are 2 independent parts, one for each index of `pop`. A program takes and returns all parts, laid end to end along the dimension named above; an argument that names none is the same for every part. Nothing has to cross between parts.
Inputs may be any that keep to these rules, and one draw needn't show every extreme that they name: Each row of hidden_order holds every number 0 to 255 once.
All inputs are finite; a program needn't handle non-finite values. No bound on the sum of `assigned` on one device may be relied on, other than what follows from the above.
Results may differ from a plain program's by a relative error of at most 0.012.
Values may be sent and summed in bfloat16 or wider, within the bound.
A program may use at most 384 MiB of HBM per device.

v0:
```python
import jax
import jax.numpy as jnp
import numpy as np
from jax import lax
from jax.sharding import PartitionSpec as P

BLK = 256
LEVELS = 7
IB = 64


inv_root_two = 0.7071067811865476
inv_root_tau = 0.3989422804014327


def partner(value, axis, distance):
    mask = 2**distance
    pairs = [(source, source ^ mask) for source in range(lax.axis_size(axis))]
    return lax.ppermute(value, axis, pairs)


def contract(left, right, left_dim, right_dim):
    return lax.dot_general(
        left, right, (((left_dim,), (right_dim,)), ((), ())), preferred_element_type=jnp.float32
    )


def stride_of(level_index):
    return 2**level_index if level_index < LEVELS else 0


def partner_bit(stride_size, per_device):
    return (stride_size // per_device).bit_length() - 1


def local_blocks(blocks, stride_size):
    if stride_size == 0:
        return blocks
    return blocks[:, np.arange(blocks.shape[1]) ^ stride_size]


def input_blocks(own_blocks, stride_size, per_device):
    if stride_size < per_device:
        return local_blocks(own_blocks, stride_size)
    return partner(own_blocks, "hid", partner_bit(stride_size, per_device))


def grad_blocks(own_blocks, stride_size, per_device):
    if stride_size < per_device:
        return local_blocks(own_blocks, stride_size)
    return partner(own_blocks, "hid", partner_bit(stride_size, per_device))


def route_outputs(partial_out, stride_size, per_device):
    if stride_size < per_device:
        return local_blocks(partial_out, stride_size)
    return partner(partial_out, "hid", partner_bit(stride_size, per_device))


def route_features(partial_feat, stride_size, per_device):
    if stride_size < per_device:
        return local_blocks(partial_feat, stride_size)
    return partner(
        partial_feat.astype(jnp.bfloat16), "hid", partner_bit(stride_size, per_device)
    ).astype(partial_feat.dtype)


def rank_sum(left, right, right_flipped):

    def term():
        if right_flipped:
            return contract(left, right, 1, 1)
        return jnp.dot(left, right, preferred_element_type=jnp.float32)

    return lax.psum(term(), "hid").astype(jnp.bfloat16)


def gelu_slope(values):
    return (
        0.5 * (1.0 + lax.erf(values * inv_root_two))
        + values * jnp.exp(-0.5 * values * values) * inv_root_tau
    )


def on_device(
    tokens,
    teacher,
    assigned,
    bfly_in,
    bfly_out,
    low_in_a,
    low_in_b,
    low_out_a,
    low_out_b,
    hidden_order,
):
    row_count = tokens.shape[0]
    per_device = bfly_in.shape[0]
    loss_scale = (row_count * lax.axis_size("tok")) ** (-0.5)
    own_input = tokens.reshape(row_count, per_device, IB)
    pre_act = jnp.zeros((row_count, per_device, BLK), jnp.float32)
    fetched = []
    for level_index in range(LEVELS + 1):
        stride_size = stride_of(level_index)
        source = input_blocks(own_input, stride_size, per_device)
        fetched.append(source)
        pre_act = pre_act + jnp.einsum(
            "rbi,bio->rbo", source, bfly_in[:, level_index], preferred_element_type=jnp.float32
        )
    low_first = rank_sum(tokens, low_in_a, False)
    pre_act = pre_act + jnp.dot(low_first, low_in_b, preferred_element_type=jnp.float32).reshape(
        row_count, per_device, BLK
    )
    activated = jax.nn.gelu(pre_act, approximate=False)
    hidden = jnp.take_along_axis(activated, hidden_order[None], axis=2).astype(jnp.bfloat16)
    hidden_flat = hidden.reshape(row_count, per_device * BLK)
    out_bfly = jnp.zeros((row_count, per_device, IB), jnp.float32)
    for level_index in range(LEVELS + 1):
        partial_out = jnp.einsum(
            "rbo,boi->rbi", hidden, bfly_out[:, level_index], preferred_element_type=jnp.float32
        )
        out_bfly = out_bfly + route_outputs(partial_out, stride_of(level_index), per_device)
    low_second = rank_sum(hidden_flat, low_out_a, False)
    student = (
        out_bfly.reshape(row_count, per_device * IB)
        + jnp.dot(low_second, low_out_b, preferred_element_type=jnp.float32)
    ).astype(jnp.bfloat16)
    residual_grad = (
        assigned[:, None].astype(jnp.float32)
        * (student.astype(jnp.float32) - teacher.astype(jnp.float32))
    ).astype(jnp.bfloat16)
    grad_own = residual_grad.reshape(row_count, per_device, IB)
    hid_bfly = jnp.zeros((row_count, per_device, BLK), jnp.float32)
    out_tiles = []
    for level_index in range(LEVELS + 1):
        source = grad_blocks(grad_own, stride_of(level_index), per_device)
        hid_bfly = hid_bfly + jnp.einsum(
            "rbi,boi->rbo", source, bfly_out[:, level_index], preferred_element_type=jnp.float32
        )
        out_tiles.append(
            jnp.einsum("rbo,rbi->boi", hidden, source, preferred_element_type=jnp.float32)
            * loss_scale
        )
    grad_second = rank_sum(residual_grad, low_out_b, True)
    hidden_grad = hid_bfly.reshape(row_count, per_device * BLK) + contract(
        grad_second, low_out_a, 1, 1
    )
    inverse_order = jnp.argsort(hidden_order, axis=1)
    act_grad = jnp.take_along_axis(
        hidden_grad.reshape(row_count, per_device, BLK), inverse_order[None], axis=2
    )
    pre_grad = (act_grad * gelu_slope(pre_act)).astype(jnp.bfloat16)
    pre_flat = pre_grad.reshape(row_count, per_device * BLK)
    feat_bfly = jnp.zeros((row_count, per_device, IB), jnp.float32)
    for level_index in range(LEVELS + 1):
        partial_feat = jnp.einsum(
            "rbo,bio->rbi", pre_grad, bfly_in[:, level_index], preferred_element_type=jnp.float32
        )
        feat_bfly = feat_bfly + route_features(partial_feat, stride_of(level_index), per_device)
    in_tiles = []
    for level_index in range(LEVELS + 1):
        in_tiles.append(
            jnp.einsum(
                "rbi,rbo->bio", fetched[level_index], pre_grad, preferred_element_type=jnp.float32
            )
            * loss_scale
        )
    grad_first = rank_sum(pre_flat, low_in_b, True)
    grad_tokens = (
        feat_bfly.reshape(row_count, per_device * IB) + contract(grad_first, low_in_a, 1, 1)
    ).astype(jnp.bfloat16)
    summed = (
        lax.psum_scatter(jnp.stack(in_tiles, axis=1), "tok", scatter_dimension=3, tiled=True),
        lax.psum_scatter(jnp.stack(out_tiles, axis=1), "tok", scatter_dimension=2, tiled=True),
        lax.psum_scatter(
            contract(tokens, grad_first, 0, 0) * loss_scale, "tok", scatter_dimension=1, tiled=True
        ),
        lax.psum_scatter(
            contract(low_first, pre_flat, 0, 0) * loss_scale, "tok", scatter_dimension=0, tiled=True
        ),
        lax.psum_scatter(
            contract(hidden_flat, grad_second, 0, 0) * loss_scale,
            "tok",
            scatter_dimension=1,
            tiled=True,
        ),
        lax.psum_scatter(
            contract(low_second, residual_grad, 0, 0) * loss_scale,
            "tok",
            scatter_dimension=0,
            tiled=True,
        ),
    )
    return (student, grad_tokens, summed[0], summed[1], summed[2], summed[3], summed[4], summed[5])


def solution(mesh):
    placed = (
        P(("pop", "tok"), "hid"),
        P(("pop", "tok"), "hid"),
        P(("pop", "tok")),
        P(("pop", "hid"), None, None, None),
        P(("pop", "hid"), None, None, None),
        P(("pop", "hid"), None),
        P("pop", "hid"),
        P(("pop", "hid"), None),
        P("pop", "hid"),
        P("hid", None),
    )
    return jax.shard_map(
        on_device,
        mesh=mesh,
        in_specs=placed,
        out_specs=(
            P(("pop", "tok"), "hid"),
            P(("pop", "tok"), "hid"),
            P(("pop", "hid"), None, None, "tok"),
            P(("pop", "hid"), None, "tok", None),
            P(("pop", "hid"), "tok"),
            P(("pop", "tok"), "hid"),
            P(("pop", "hid"), "tok"),
            P(("pop", "tok"), "hid"),
        ),
        check_vma=False,
    )
```

profile of v0, /device:TPU:0, one launch (start us, length us, event | category | flops | bytes accessed | tf_op | source)
XLA Modules:
  0.0 1211.0 jit_solution(8584214798929605454)
XLA Ops:
  20.7 134.3 %all-reduce.4 = bf16[768,512]{1,0:T(8,128)(2,1)S(1)} all-reduce(f32[768,512]{1,0:T(8,128)} %fusion.229), channel_id=1, replica_groups=mesh['pop'=2,'hid'=8,'tok'=2] {'hid'}, use_global_device_ids=true, to_apply=%region_0.0 | all-reduce | flops 393216 | bytes 2359296 | tf_op jit(solution)/shard_map/psum | solution.py:75
  160.6 7.6 fusion.164
  168.2 7.5 fusion.48
  175.7 7.6 fusion.44
  183.3 6.6 fusion.235
  189.9 7.5 fusion.40
  199.2 7.9 fusion.36
  210.5 8.0 fusion.172
  218.5 7.9 fusion.169
  226.4 46.1 %fusion.1 = (bf16[768,16,256]{0,2,1:T(8,128)(2,1)}, f32[768,16,256]{0,2,1:T(8,128)}) fusion(f32[768,16,256]{0,2,1:T(8,128)} %bitcast.501, f32[16,256,768]{2,1,0:T(8,128)} %fusion.164, bf16[768,16,64]{0,2,1:T(8,128)(2,1)} %collective-permute-done.2, bf16[16,8,64,256]{3,2,1,0:T(8,128)(2,1)} %param.47, f32[16,256,768]{2,1,0:T(8,128)} %fusion.169, ...), kind=kOutput, calls=%fused_computation.21 | convolution fusion | flops 632291328 | bytes 121634816 | tf_op jit(solution)/shard_map/rbi,bio->rbo/dot_general | solution.py:107
  272.6 76.1 %gather_fusion.16 = bf16[4096,768]{1,0:T(8,128)(2,1)} fusion(bf16[768,16,256]{0,2,1:T(8,128)(2,1)} %get-tuple-element.29, s32[4096]{0:T(1024)S(1)} %bitcast.477), kind=kCustom, calls=%fused_computation.clone | custom fusion | bytes 12615680 | tf_op jit(solution)/shard_map/jit(take_along_axis)/gather | solution.py:115
  348.6 4.8 bitcast_convert_fusion
  377.6 5.8 convolution_bitcast_fusion.9
  388.0 5.8 convolution_bitcast_fusion.8
  398.2 5.8 convolution_bitcast_fusion.7
  408.6 157.5 %all-reduce.5 = bf16[768,512]{1,0:T(8,128)(2,1)S(1)} all-reduce(f32[768,512]{1,0:T(8,128)S(1)} %fusion.230), channel_id=1, replica_groups=mesh['pop'=2,'hid'=8,'tok'=2] {'hid'}, use_global_device_ids=true, to_apply=%region_1.3 | all-reduce | flops 393216 | bytes 2359296 | tf_op jit(solution)/shard_map/psum | solution.py:75
  570.3 11.3 bitcast_add_fusion.6
  606.5 7.4 fusion.143
  613.9 117.6 %all-reduce.6 = bf16[768,512]{1,0:T(8,128)(2,1)S(1)} all-reduce(f32[768,512]{1,0:T(8,128)} %fusion.231), channel_id=1, replica_groups=mesh['pop'=2,'hid'=8,'tok'=2] {'hid'}, use_global_device_ids=true, to_apply=%region_2.0 | all-reduce | flops 393216 | bytes 2359296 | tf_op jit(solution)/shard_map/psum | solution.py:75
  731.6 8.0 fusion.20
  739.7 6.4 fusion.24
  746.0 6.4 fusion.28
  752.5 6.4 fusion.32
  758.8 7.8 fusion.151
  766.6 7.8 fusion.154
  774.5 33.3 %add_add_fusion = f32[16,768,256]{1,2,0:T(8,128)} fusion(f32[16,768,256]{1,2,0:T(8,128)} %fusion.143, f32[16,768,256]{1,2,0:T(8,128)} %fusion.151, f32[16,768,256]{1,2,0:T(8,128)} %fusion.154, f32[16,768,256]{1,2,0:T(8,128)} %fusion.20, f32[16,768,256]{1,2,0:T(8,128)} %fusion.24, f32[16,768,256]{1,2,0:T(8,128)} %fusion.32, f32[16,768,256]{1,2,0:T(8,128)} %fusion.28, ...), kind=kOutput, calls=%fused_computation.34 | convolution fusion | flops 424673280 | bytes 102760448 | tf_op jit(solution)/shard_map/rbi,boi->rbo/dot_general | solution.py:137
  807.8 12.6 %copy.125 = f32[768,4096]{1,0:T(8,128)} copy(f32[768,4096]{0,1:T(8,128)} %bitcast.496) | data formatting | bytes 25165824 | tf_op jit(solution)/shard_map/reshape | solution.py:145
  820.4 10.6 convolution_add_fusion
  831.1 12.7 %copy.188 = f32[768,4096]{0,1:T(8,128)} copy(f32[768,4096]{1,0:T(8,128)} %convolution_add_fusion) | data formatting | bytes 25165824 | tf_op jit(solution)/shard_map/reshape | solution.py:150
  843.7 75.2 %gather_fusion.17 = f32[4096,768]{1,0:T(8,128)} fusion(f32[768,16,256]{0,2,1:T(8,128)} %bitcast.475, s32[4096]{0:T(1024)S(1)} %bitcast.476), kind=kCustom, calls=%fused_computation.1.clone | custom fusion | bytes 25198592 | tf_op jit(solution)/shard_map/jit(take_along_axis)/gather | solution.py:149
  918.9 9.5 fusion.7
  931.0 4.7 fusion.232
  935.7 77.9 %all-reduce.7 = bf16[768,512]{1,0:T(8,128)(2,1)S(1)} all-reduce(f32[768,512]{1,0:T(8,128)} %fusion.232), channel_id=1, replica_groups=mesh['pop'=2,'hid'=8,'tok'=2] {'hid'}, use_global_device_ids=true, to_apply=%region_4.0 | all-reduce | flops 393216 | bytes 2359296 | tf_op jit(solution)/shard_map/psum | solution.py:75
  1018.2 6.3 fusion.97
  1024.5 6.2 fusion.106
  1053.2 6.4 fusion.61
  1059.6 7.5 fusion.70
  1093.5 9.4 convolution_multiply_fusion
  1104.1 8.5 convolution_multiply_fusion.1
  1112.6 6.1 fusion.54
  1132.6 5.2 gather_fusion.12
  1137.7 6.0 convolution_bitcast_fusion.2
  1148.1 6.8 convolution_bitcast_fusion.1
  1154.9 5.2 gather_fusion.14
  1160.2 5.8 convolution_bitcast_fusion
  1173.2 10.5 bitcast_add_fusion.4
  1194.3 4.9 copy.153
  1199.2 4.8 copy.152
  (215 shorter events, 183.9 us)
Async XLA Ops:
  7.2 558.9 %copy-start = (bf16[512,1024]{1,0:T(8,128)(2,1)S(1)}, bf16[512,1024]{1,0:T(8,128)(2,1)}, u32[]{:S(2)}) copy-start(bf16[512,1024]{1,0:T(8,128)(2,1)} %param.52) | copy-start | bytes 3145732
  7.2 200.6 %sort.19.cloned.1.call-start = ((), (), s32[]{:S(2)}) async-start(), calls=%async_computation.12 | async-start | bytes 98336 | tf_op jit(solution)/shard_map/jit(argsort)/sort | solution.py:148
  9.0 188.4 %copy-start.5 = (bf16[768,1024]{0,1:T(8,128)(2,1)}, bf16[768,1024]{0,1:T(8,128)(2,1)S(1)}, u32[]{:S(2)}) copy-start(bf16[768,1024]{0,1:T(8,128)(2,1)S(1)} %copy.97) | copy-start | bytes 4718596
  9.0 217.4 %collective-permute-start.2 = (bf16[768,16,64]{0,2,1:T(8,128)(2,1)S(1)}, bf16[768,16,64]{0,2,1:T(8,128)(2,1)}, u32[]{:S(2)}, u32[]{:S(2)}) collective-permute-start(bf16[768,16,64]{0,2,1:T(8,128)(2,1)S(1)} %bitcast.478), channel_id=1, source_target_pairs={{0,8},{2,10},{4,12},{6,14},{8,0},{10,2},{12,4},{14,6},{1,9},{3,11}... | collective-permute-start | bytes 4718600 | tf_op jit(solution)/shard_map/ppermute | solution.py:19
  13.1 205.3 %collective-permute-start.1 = (bf16[768,16,64]{0,2,1:T(8,128)(2,1)S(1)}, bf16[768,16,64]{0,2,1:T(8,128)(2,1)}, u32[]{:S(2)}, u32[]{:S(2)}) collective-permute-start(bf16[768,16,64]{0,2,1:T(8,128)(2,1)S(1)} %bitcast.479), channel_id=1, source_target_pairs={{0,4},{2,6},{4,0},{6,2},{8,12},{10,14},{12,8},{14,10},{1,5},{3,7},... | collective-permute-start | bytes 4718600 | tf_op jit(solution)/shard_map/ppermute | solution.py:19
  14.7 195.7 %collective-permute-start = (bf16[768,16,64]{0,2,1:T(8,128)(2,1)S(1)}, bf16[768,16,64]{0,2,1:T(8,128)(2,1)}, u32[]{:S(2)}, u32[]{:S(2)}) collective-permute-start(bf16[768,16,64]{0,2,1:T(8,128)(2,1)S(1)} %bitcast.480), channel_id=1, source_target_pairs={{0,2},{2,0},{4,6},{6,4},{8,10},{10,8},{12,14},{14,12},{1,3},{3,1},... | collective-permute-start | bytes 4718600 | tf_op jit(solution)/shard_map/ppermute | solution.py:19
  16.8 138.2 %copy-start.43 = (s32[16]{0:T(128)S(1)}, s32[16]{0:T(128)}, u32[]{:S(2)}) copy-start(s32[16]{0:T(128)} %constant.131) | copy-start | bytes 196
  16.9 138.2 %copy-start.46 = (s32[16]{0:T(128)S(1)}, s32[16]{0:T(128)}, u32[]{:S(2)}) copy-start(s32[16]{0:T(128)} %constant.130) | copy-start | bytes 196
  16.9 1174.9 %reduce-scatter.11.cloned.1.call-start = ((), (), s32[]{:S(2)}) async-start(), calls=%async_computation.8 | async-start | bytes 3145728 | tf_op jit(solution)/shard_map/reduce_scatter | solution.py:175
  20.7 136.2 %copy-start.44 = (s32[16]{0:T(128)S(1)}, s32[16]{0:T(128)}, u32[]{:S(2)}) copy-start(s32[16]{0:T(128)} %constant.129) | copy-start | bytes 196
  20.7 136.2 %copy-start.45 = (s32[16]{0:T(128)S(1)}, s32[16]{0:T(128)}, u32[]{:S(2)}) copy-start(s32[16]{0:T(128)} %constant.128) | copy-start | bytes 196
  155.1 28.2 %copy-start.33 = (bf16[768,512]{1,0:T(8,128)(2,1)}, bf16[768,512]{1,0:T(8,128)(2,1)S(1)}, u32[]{:S(2)}) copy-start(bf16[768,512]{1,0:T(8,128)(2,1)S(1)} %all-reduce.4) | copy-start | bytes 2359300
  155.1 42.3 %copy-start.38 = (s32[1024]{0:T(1024)}, s32[1024]{0:T(1024)S(1)}, u32[]{:S(2)}) copy-start(s32[1024]{0:T(1024)S(1)} %get-tuple-element.31) | copy-start | bytes 12292
  160.6 7.6 copy-start.17
  168.2 7.5 copy-start.14
  175.7 7.6 copy-start.47
  183.3 6.6 copy-start.12
  199.2 7.9 copy-start.35
  199.2 8.0 copy-start.42
  353.4 16.9 %copy-start.2 = (bf16[768,16,256]{0,2,1:T(8,128)(2,1)}, bf16[768,16,256]{0,2,1:T(8,128)(2,1)S(1)}, u32[]{:S(2)}) copy-start(bf16[768,16,256]{0,2,1:T(8,128)(2,1)S(1)} %bitcast_convert_fusion) | copy-start | bytes 18874372
  359.7 7.2 copy-start.28
  362.5 206.2 %collective-permute-start.5 = (f32[768,16,64]{0,2,1:T(8,128)}, f32[768,16,64]{0,2,1:T(8,128)}, u32[]{:S(2)}, u32[]{:S(2)}) collective-permute-start(f32[768,16,64]{0,2,1:T(8,128)} %convolution_bitcast_fusion.4), channel_id=1, source_target_pairs={{0,8},{2,10},{4,12},{6,14},{8,0},{10,2},{12,4},{14,6},{1,9},{3,11}... | collective-permute-start | bytes 9437192 | tf_op jit(solution)/shard_map/ppermute | solution.py:19
  363.2 205.6 %collective-permute-start.4 = (f32[768,16,64]{0,2,1:T(8,128)}, f32[768,16,64]{0,2,1:T(8,128)}, u32[]{:S(2)}, u32[]{:S(2)}) collective-permute-start(f32[768,16,64]{0,2,1:T(8,128)} %convolution_bitcast_fusion.5), channel_id=1, source_target_pairs={{0,4},{2,6},{4,0},{6,2},{8,12},{10,14},{12,8},{14,10},{1,5},{3,7},... | collective-permute-start | bytes 9437192 | tf_op jit(solution)/shard_map/ppermute | solution.py:19
  364.7 204.0 %collective-permute-start.3 = (f32[768,16,64]{0,2,1:T(8,128)}, f32[768,16,64]{0,2,1:T(8,128)}, u32[]{:S(2)}, u32[]{:S(2)}) collective-permute-start(f32[768,16,64]{0,2,1:T(8,128)} %convolution_bitcast_fusion.6), channel_id=1, source_target_pairs={{0,2},{2,0},{4,6},{6,4},{8,10},{10,8},{12,14},{14,12},{1,3},{3,1},... | collective-permute-start | bytes 9437192 | tf_op jit(solution)/shard_map/ppermute | solution.py:19
  566.1 15.6 %copy-start.26 = (bf16[768,512]{1,0:T(8,128)(2,1)}, bf16[768,512]{1,0:T(8,128)(2,1)S(1)}, u32[]{:S(2)}) copy-start(bf16[768,512]{1,0:T(8,128)(2,1)S(1)} %all-reduce.5) | copy-start | bytes 2359300
  602.5 171.9 %collective-permute-start.8 = (bf16[768,16,64]{0,2,1:T(8,128)(2,1)S(1)}, bf16[768,16,64]{0,2,1:T(8,128)(2,1)}, u32[]{:S(2)}, u32[]{:S(2)}) collective-permute-start(bf16[768,16,64]{0,2,1:T(8,128)(2,1)S(1)} %bitcast.491), channel_id=1, source_target_pairs={{0,8},{2,10},{4,12},{6,14},{8,0},{10,2},{12,4},{14,6},{1,9},{3,11}... | collective-permute-start | bytes 4718600 | tf_op jit(solution)/shard_map/ppermute | solution.py:19
  603.1 155.7 %collective-permute-start.7 = (bf16[768,16,64]{0,2,1:T(8,128)(2,1)S(1)}, bf16[768,16,64]{0,2,1:T(8,128)(2,1)}, u32[]{:S(2)}, u32[]{:S(2)}) collective-permute-start(bf16[768,16,64]{0,2,1:T(8,128)(2,1)S(1)} %bitcast.492), channel_id=1, source_target_pairs={{0,4},{2,6},{4,0},{6,2},{8,12},{10,14},{12,8},{14,10},{1,5},{3,7},... | collective-permute-start | bytes 4718600 | tf_op jit(solution)/shard_map/ppermute | solution.py:19
  604.6 162.0 %collective-permute-start.6 = (bf16[768,16,64]{0,2,1:T(8,128)(2,1)S(1)}, bf16[768,16,64]{0,2,1:T(8,128)(2,1)}, u32[]{:S(2)}, u32[]{:S(2)}) collective-permute-start(bf16[768,16,64]{0,2,1:T(8,128)(2,1)S(1)} %bitcast.493), channel_id=1, source_target_pairs={{0,2},{2,0},{4,6},{6,4},{8,10},{10,8},{12,14},{14,12},{1,3},{3,1},... | collective-permute-start | bytes 4718600 | tf_op jit(solution)/shard_map/ppermute | solution.py:19
  731.6 8.1 copy-start.8
  731.6 8.1 copy-start.19
  831.1 12.7 %copy-start.4 = (s32[2,2,8,128]{3,1,2,0:T(2,128)S(1)}, s32[2,2,8,128]{3,1,2,0:T(2,128)}, u32[]{:S(2)}) copy-start(s32[2,2,8,128]{3,1,2,0:T(2,128)} %copy.206) | copy-start | bytes 49156
  843.7 75.2 %copy-start.37 = (pred[16,256]{1,0:T(8,128)(4,1)S(1)}, pred[16,256]{1,0:T(8,128)(4,1)}, u32[]{:S(2)}) copy-start(pred[16,256]{1,0:T(8,128)(4,1)} %and_bitcast_fusion) | copy-start | bytes 12292
  918.9 12.1 %copy-start.48 = (bf16[512,4096]{1,0:T(8,128)(2,1)S(1)}, bf16[512,4096]{1,0:T(8,128)(2,1)}, u32[]{:S(2)}) copy-start(bf16[512,4096]{1,0:T(8,128)(2,1)} %param.50) | copy-start | bytes 12582916
  1013.6 10.9 copy-start.29
  1017.7 176.6 %reduce-scatter.9.cloned.1.call-start = ((), (), s32[]{:S(2)}) async-start(), calls=%async_computation.7 | async-start | bytes 12582912 | tf_op jit(solution)/shard_map/reduce_scatter | solution.py:174
  1018.1 12.5 %slice-start = ((s8[6291456]{0:T(1024)(128)(4,1)}), s8[4194304]{0:T(1024)(128)(4,1)S(1)}, s32[]{:S(2)}) async-start(s8[6291456]{0:T(1024)(128)(4,1)} %bitcast.467), calls=%async_computation.14 | async-start | bytes 8388608
  1052.9 6.7 copy-start.15
  1052.9 146.2 %reduce-scatter.7.cloned.1.call-start = ((), (), s32[]{:S(2)}) async-start(), calls=%async_computation.6 | async-start | bytes 12582912 | tf_op jit(solution)/shard_map/reduce_scatter | solution.py:173
  1053.2 14.0 %slice-start.2 = ((s8[6291456]{0:T(1024)(128)(4,1)}), s8[4194304]{0:T(1024)(128)(4,1)S(1)}, s32[]{:S(2)}) async-start(s8[6291456]{0:T(1024)(128)(4,1)} %bitcast.471), calls=%async_computation.16 | async-start | bytes 8388608
  1059.6 7.5 slice-start.3
  1059.6 7.5 copy-start.13
  1089.5 114.4 %reduce-scatter.17.cloned.1.call-start = ((), (), s32[]{:S(2)}) async-start(), calls=%async_computation.11 | async-start | bytes 3145728 | tf_op jit(solution)/shard_map/reduce_scatter | solution.py:187
  1093.5 110.5 %reduce-scatter.15.cloned.1.call-start = ((), (), s32[]{:S(2)}) async-start(), calls=%async_computation.10 | async-start | bytes 12582912 | tf_op jit(solution)/shard_map/reduce_scatter | solution.py:181
  1103.0 101.0 %reduce-scatter.13.cloned.1.call-start = ((), (), s32[]{:S(2)}) async-start(), calls=%async_computation.9 | async-start | bytes 12582912 | tf_op jit(solution)/shard_map/reduce_scatter | solution.py:178
  1118.8 54.4 %collective-permute-start.11 = (bf16[768,16,64]{0,2,1:T(8,128)(2,1)}, bf16[768,16,64]{0,2,1:T(8,128)(2,1)}, u32[]{:S(2)}, u32[]{:S(2)}) collective-permute-start(bf16[768,16,64]{0,2,1:T(8,128)(2,1)} %fusion.54), channel_id=1, source_target_pairs={{0,8},{2,10},{4,12},{6,14},{8,0},{10,2},{12,4},{14,6},{1,9},{3,11}... | collective-permute-start | bytes 4718600 | tf_op jit(solution)/shard_map/ppermute | solution.py:19
  1122.2 51.0 %collective-permute-start.10 = (bf16[768,16,64]{0,2,1:T(8,128)(2,1)}, bf16[768,16,64]{0,2,1:T(8,128)(2,1)}, u32[]{:S(2)}, u32[]{:S(2)}) collective-permute-start(bf16[768,16,64]{0,2,1:T(8,128)(2,1)} %fusion.53), channel_id=1, source_target_pairs={{0,4},{2,6},{4,0},{6,2},{8,12},{10,14},{12,8},{14,10},{1,5},{3,7},... | collective-permute-start | bytes 4718600 | tf_op jit(solution)/shard_map/ppermute | solution.py:19
  1126.9 46.4 %collective-permute-start.9 = (bf16[768,16,64]{0,2,1:T(8,128)(2,1)}, bf16[768,16,64]{0,2,1:T(8,128)(2,1)}, u32[]{:S(2)}, u32[]{:S(2)}) collective-permute-start(bf16[768,16,64]{0,2,1:T(8,128)(2,1)} %fusion.52), channel_id=1, source_target_pairs={{0,2},{2,0},{4,6},{6,4},{8,10},{10,8},{12,14},{14,12},{1,3},{3,1},... | collective-permute-start | bytes 4718600 | tf_op jit(solution)/shard_map/ppermute | solution.py:19
  1194.3 9.7 copy-start.1
  (26 other events, 104.2 us)
Sparse Core Ops, SparseCore 0:
  17.0 2.5 sort.21.cloned.1.call-done
  1017.8 8.5 reduce-scatter.10
  1053.0 15.8 reduce-scatter.8
  1089.7 15.0 reduce-scatter.6
  1107.5 10.8 reduce-scatter.16
  1121.1 17.9 reduce-scatter.14
  1142.1 18.0 reduce-scatter.12
  (1 shorter events, 0.0 us)
where the time goes:
time: 1220 us; the launch traced here: 1210 us
  blocking collectives  487 us (40%)
  matrix products  403 us (33%)
  local copies, waits for them, and re-layouts  261 us (21%)
  other arithmetic  26 us (2%)
  starting transfers between devices  19.2 us (2%)
  between operations  14.9 us (1%)
    psum x4, blocking collectives, rank_sum(): return lax.psum(term(), 'hid').astype(jnp.bfloat16)  487 us
    dot_general x8, matrix products, on_device(): jnp.einsum('rbi,bio->rbo', source, bfly_in[:, level_index], preferred_ele...  100 us
    dot_general x8, matrix products, on_device(): jnp.einsum('rbi,boi->rbo', source, bfly_out[:, level_index], preferred_el...  83.6 us
    gather x1, local copies, waits for them, and re-layouts, on_device(): jnp.take_along_axis(activated, hidden_order[None], axis=2)  76.1 us
    gather x1, local copies, waits for them, and re-layouts, on_device(): jnp.take_along_axis(hidden_grad.reshape(row_count, per_device, BLK), inve...  75.2 us
    gather x16, local copies, waits for them, and re-layouts, local_blocks(): return blocks[:, np.arange(blocks.shape[1]) ^ stride_size]  52 us
    dot_general x8, matrix products, on_device(): jnp.einsum('rbo,bio->rbi', pre_grad, bfly_in[:, level_index], preferred_e...  46.4 us
    dot_general x8, matrix products, contract(): lax.dot_general(left, right, (((left_dim,), (right_dim,)), ((), ())), pre...  44.4 us
  transfers between devices with their start and end apart: 18, of which 0 were waited for; matrix products, arithmetic and copies ran while one was open for 29% of the time, Pallas kernels for 0%

commit v1 on v0

v1 whole, which is shorter than its diff:
```python
import functools

import jax
import jax.numpy as jnp
from jax import lax
from jax.experimental import pallas as pl
from jax.experimental.pallas import tpu as pltpu
from jax.sharding import PartitionSpec as P

BLK = 256
LEVELS = 7
IB = 64
PAIR_IN = 2 * IB
PAIR_HID = 2 * BLK
SOURCES = LEVELS
LEVEL_ORDER = (LEVELS,) + tuple(range(1, LEVELS))
WIDE = SOURCES * PAIR_IN
VMEM_BYTES = 52 * 2**20

inv_root_two = 0.7071067811865476
inv_root_tau = 0.3989422804014327


def partner(value, axis, mask):
    pairs = [(source, source ^ mask) for source in range(lax.axis_size(axis))]
    return lax.ppermute(value, axis, pairs)


def dot(left, right, left_dim, right_dim):
    return lax.dot_general(
        left, right, (((left_dim,), (right_dim,)), ((), ())), preferred_element_type=jnp.float32
    )


def hid_sum(value):
    devices = lax.axis_size("hid")
    place = lax.axis_index("hid")
    masks = [2**bit for bit in range(devices.bit_length() - 1)]
    for mask in masks:
        low, high = jnp.split(value, 2, axis=0)
        upper = (place & mask) != 0
        kept = jnp.where(upper, high, low)
        sent = jnp.where(upper, low, high).astype(jnp.bfloat16)
        value = kept + partner(sent, "hid", mask).astype(jnp.float32)
    value = value.astype(jnp.bfloat16)
    for mask in reversed(masks):
        other = partner(value, "hid", mask)
        upper = (place & mask) != 0
        value = jnp.concatenate(
            [jnp.where(upper, other, value), jnp.where(upper, value, other)], axis=0
        )
    return value


def pair_weights(tiles):
    pairs = tiles.reshape((tiles.shape[0] // 2, 2) + tiles.shape[1:])
    straight = jnp.concatenate([pairs[:, :, LEVELS:], pairs[:, :, 1:LEVELS]], axis=2)
    cross = jnp.concatenate([pairs[:, :, :1], jnp.zeros_like(pairs[:, :, 1:LEVELS])], axis=2)
    return straight, cross


def input_weights(bfly_in):
    straight, cross = pair_weights(bfly_in)
    upper = jnp.concatenate([straight[:, 0], cross[:, 1]], axis=-1)
    lower = jnp.concatenate([cross[:, 0], straight[:, 1]], axis=-1)
    both = jnp.concatenate([upper, lower], axis=-2)
    return both.reshape(both.shape[0], WIDE, PAIR_HID)


def output_weights(bfly_out):
    straight, cross = pair_weights(bfly_out)
    upper = jnp.concatenate([straight[:, 0], cross[:, 0]], axis=-1)
    lower = jnp.concatenate([cross[:, 1], straight[:, 1]], axis=-1)
    return jnp.concatenate([upper, lower], axis=-2)


def order_matrix(order_ref, half):
    order = order_ref[0, half : half + 1, :]
    return (lax.broadcasted_iota(jnp.int32, (BLK, BLK), 0) == order).astype(jnp.bfloat16)


def widen(refs):
    return jnp.concatenate([ref[...] for ref in refs], axis=1)


def level_columns(weight_ref):
    return jnp.concatenate([weight_ref[0, source] for source in range(SOURCES)], axis=1)


def spread(result, local_count, total_ref, remote_refs):
    pair = pl.program_id(0)

    @pl.when(pair == 0)
    def _():
        total_ref[...] = jnp.zeros_like(total_ref)

    for source in range(SOURCES):
        part = result[:, source * PAIR_IN : (source + 1) * PAIR_IN]
        if source <= local_count:
            target = pair ^ (0 if source == 0 else 2 ** (source - 1))
            columns = pl.ds(pl.multiple_of(target * PAIR_IN, PAIR_IN), PAIR_IN)
            total_ref[:, columns] += part
        else:
            remote_refs[source - local_count - 1][...] = part.astype(jnp.bfloat16)


def accumulate(ref, part):
    @pl.when(pl.program_id(0) == 0)
    def _():
        ref[...] = part

    @pl.when(pl.program_id(0) > 0)
    def _():
        ref[...] += part


def forward_kernel(local_count, *refs):
    sources = refs[:SOURCES]
    in_ref, out_ref, first_ref, low_in_b_ref, low_out_a_ref, order_ref = refs[SOURCES : SOURCES + 6]
    hidden_ref, slope_ref, total_ref, second_ref = refs[SOURCES + 6 : SOURCES + 10]
    remote = refs[SOURCES + 10 :]
    pre_act = dot(widen(sources), in_ref[0], 1, 0) + dot(first_ref[...], low_in_b_ref[...], 1, 0)
    cumulative = 0.5 * (1.0 + lax.erf(pre_act * inv_root_two))
    density = jnp.exp(-0.5 * pre_act * pre_act) * inv_root_tau
    activated = (pre_act * cumulative).astype(jnp.bfloat16)
    slope = (cumulative + pre_act * density).astype(jnp.bfloat16)
    for half in range(2):
        matrix = order_matrix(order_ref, half)
        columns = slice(half * BLK, (half + 1) * BLK)
        hidden_ref[:, columns] = dot(activated[:, columns], matrix, 1, 0).astype(jnp.bfloat16)
        slope_ref[:, columns] = dot(slope[:, columns], matrix, 1, 0).astype(jnp.bfloat16)
    hidden = hidden_ref[...]
    spread(dot(hidden, level_columns(out_ref), 1, 0), local_count, total_ref, remote)
    accumulate(second_ref, dot(hidden, low_out_a_ref[...], 1, 0))


def backward_kernel(local_count, *refs):
    sources = refs[:SOURCES]
    in_ref, out_ref, second_ref, low_in_b_ref, low_out_a_ref, order_ref, slope_ref = refs[
        SOURCES : SOURCES + 7
    ]
    pre_grad_ref, total_ref, first_ref = refs[SOURCES + 7 : SOURCES + 10]
    remote = refs[SOURCES + 10 :]
    hidden_grad = dot(widen(sources), level_columns(out_ref), 1, 1) + dot(
        second_ref[...], low_out_a_ref[...], 1, 1
    )
    ordered = (hidden_grad * slope_ref[...].astype(jnp.float32)).astype(jnp.bfloat16)
    for half in range(2):
        matrix = order_matrix(order_ref, half)
        columns = slice(half * BLK, (half + 1) * BLK)
        pre_grad_ref[:, columns] = dot(ordered[:, columns], matrix, 1, 1).astype(jnp.bfloat16)
    pre_grad = pre_grad_ref[...]
    spread(dot(pre_grad, in_ref[0], 1, 1), local_count, total_ref, remote)
    accumulate(first_ref, dot(pre_grad, low_in_b_ref[...], 1, 1))


def keep_and_send(lower, upper, keep_ref, send_ref, where=...):
    second = lax.axis_index("tok") == 1
    keep_ref[where] = jnp.where(second, upper, lower)
    send_ref[where] = jnp.where(second, lower, upper).astype(jnp.bfloat16)


def tile_places():
    for half in range(2):
        yield half, 0, 0, 1 - half
        for source, level in enumerate(LEVEL_ORDER):
            yield half, level, source, half


def grad_in_kernel(scale, *refs):
    sources = refs[:SOURCES]
    pre_grad_ref, first_ref, tile_keep, tile_send, low_keep, low_send = refs[SOURCES:]
    pre_grad = pre_grad_ref[...]
    tiles = dot(widen(sources), pre_grad, 0, 0) * scale
    for half, level, source, side in tile_places():
        start = source * PAIR_IN + side * IB
        tile = tiles[start : start + IB, half * BLK : (half + 1) * BLK]
        keep_and_send(
            tile[:, : BLK // 2], tile[:, BLK // 2 :], tile_keep, tile_send, (half, level)
        )
    low = dot(first_ref[...], pre_grad, 0, 0) * scale
    middle = low.shape[0] // 2
    keep_and_send(low[:middle], low[middle:], low_keep, low_send)


def grad_out_kernel(scale, *refs):
    sources = refs[:SOURCES]
    hidden_ref, second_ref, tile_keep, tile_send, low_keep, low_send = refs[SOURCES:]
    hidden = hidden_ref[...]
    tiles = dot(hidden, widen(sources), 0, 0) * scale
    for half, level, source, side in tile_places():
        start = source * PAIR_IN + side * IB
        tile = tiles[half * BLK : (half + 1) * BLK, start : start + IB]
        keep_and_send(tile[: BLK // 2], tile[BLK // 2 :], tile_keep, tile_send, (half, level))
    low = dot(hidden, second_ref[...], 0, 0) * scale
    middle = low.shape[1] // 2
    keep_and_send(low[:, :middle], low[:, middle:], low_keep, low_send)


def call(kernel, pairs, in_specs, out_specs, out_shape, args, flops):
    size = sum(a.size * a.dtype.itemsize for a in args) + sum(
        s.size * s.dtype.itemsize for s in out_shape
    )
    return pl.pallas_call(
        kernel,
        grid=(pairs,),
        in_specs=in_specs,
        out_specs=out_specs,
        out_shape=out_shape,
        compiler_params=pltpu.CompilerParams(
            vmem_limit_bytes=VMEM_BYTES, dimension_semantics=("arbitrary",)
        ),
        cost_estimate=pl.CostEstimate(flops=flops, bytes_accessed=size, transcendentals=0),
    )(*args)


def on_device(
    tokens,
    teacher,
    assigned,
    bfly_in,
    bfly_out,
    low_in_a,
    low_in_b,
    low_out_a,
    low_out_b,
    hidden_order,
):
    rows, features = tokens.shape
    per_device = bfly_in.shape[0]
    pairs = per_device // 2
    units = per_device * BLK
    rank = low_in_a.shape[1]
    loss_scale = (rows * lax.axis_size("tok")) ** (-0.5)
    local_count = per_device.bit_length() - 2
    masks = [2**level // per_device for level in range(local_count + 1, LEVELS)]
    remote_count = len(masks)
    sds = jax.ShapeDtypeStruct
    bf16, f32 = jnp.bfloat16, jnp.float32

    def exchange(values):
        return [partner(value, "hid", mask) for value, mask in zip(values, masks)]

    feature_spec = pl.BlockSpec((rows, PAIR_IN), lambda p: (0, p))
    local_specs = [
        pl.BlockSpec((rows, PAIR_IN), functools.partial(lambda s, p: (0, p ^ s), 2**level))
        for level in range(local_count)
    ]
    source_specs = [feature_spec] + local_specs + [feature_spec] * remote_count
    unit_spec = pl.BlockSpec((rows, PAIR_HID), lambda p: (0, p))
    whole_rank = pl.BlockSpec((rows, rank), lambda p: (0, 0))
    whole_features = pl.BlockSpec((rows, features), lambda p: (0, 0))
    in_spec = pl.BlockSpec((1, WIDE, PAIR_HID), lambda p: (p, 0, 0))
    out_spec = pl.BlockSpec((1, SOURCES, PAIR_HID, PAIR_IN), lambda p: (p, 0, 0, 0))
    rank_columns = pl.BlockSpec((rank, PAIR_HID), lambda p: (0, p))
    rank_rows = pl.BlockSpec((PAIR_HID, rank), lambda p: (p, 0))
    order_spec = pl.BlockSpec((1, 2, BLK), lambda p: (p, 0, 0))
    remote_shapes = [sds((rows, features), bf16)] * remote_count
    order = hidden_order.reshape(pairs, 2, BLK)
    work = 2 * rows * units

    def with_local(own, remote):
        return [own] * (1 + local_count) + remote

    low_first = hid_sum(dot(tokens, low_in_a, 1, 0))
    token_sources = with_local(tokens, exchange([tokens] * remote_count))
    w_in = input_weights(bfly_in)
    w_out = output_weights(bfly_out)

    hidden, slope, out_total, second_part, *out_remote = call(
        functools.partial(forward_kernel, local_count),
        pairs,
        source_specs + [in_spec, out_spec, whole_rank, rank_columns, rank_rows, order_spec],
        [unit_spec, unit_spec, whole_features, whole_rank] + [feature_spec] * remote_count,
        [
            sds((rows, units), bf16),
            sds((rows, units), bf16),
            sds((rows, features), f32),
            sds((rows, rank), f32),
        ]
        + remote_shapes,
        token_sources + [w_in, w_out, low_first, low_in_b, low_out_a, order],
        work * 2 * (WIDE + rank + BLK),
    )
    low_second = hid_sum(second_part)
    student_wide = out_total + dot(low_second, low_out_b, 1, 0)
    for arrived in exchange(out_remote):
        student_wide = student_wide + arrived.astype(f32)
    student = student_wide.astype(bf16)
    residual_grad = (
        assigned[:, None].astype(f32) * (student.astype(f32) - teacher.astype(f32))
    ).astype(bf16)
    grad_second = hid_sum(dot(residual_grad, low_out_b, 1, 1))
    grad_sources = with_local(residual_grad, exchange([residual_grad] * remote_count))

    pre_grad, feat_total, first_part, *feat_remote = call(
        functools.partial(backward_kernel, local_count),
        pairs,
        source_specs
        + [in_spec, out_spec, whole_rank, rank_columns, rank_rows, order_spec, unit_spec],
        [unit_spec, whole_features, whole_rank] + [feature_spec] * remote_count,
        [sds((rows, units), bf16), sds((rows, features), f32), sds((rows, rank), f32)]
        + remote_shapes,
        grad_sources + [w_in, w_out, grad_second, low_in_b, low_out_a, order, slope],
        work * 2 * (WIDE + rank + BLK // 2),
    )
    feat_arrived = exchange(feat_remote)
    grad_first = hid_sum(first_part)

    tile_in = pl.BlockSpec((2, LEVELS + 1, IB, BLK // 2), lambda p: (p, 0, 0, 0))
    low_in = pl.BlockSpec((rank // 2, PAIR_HID), lambda p: (0, p))
    tile_out = pl.BlockSpec((2, LEVELS + 1, BLK // 2, IB), lambda p: (p, 0, 0, 0))
    low_out = pl.BlockSpec((PAIR_HID, rank // 2), lambda p: (p, 0))
    tile_in_dims = (per_device, LEVELS + 1, IB, BLK // 2)
    tile_out_dims = (per_device, LEVELS + 1, BLK // 2, IB)
    kept_out = call(
        functools.partial(grad_out_kernel, loss_scale),
        pairs,
        source_specs + [unit_spec, whole_rank],
        [tile_out, tile_out, low_out, low_out],
        [
            sds(tile_out_dims, f32),
            sds(tile_out_dims, bf16),
            sds((units, rank // 2), f32),
            sds((units, rank // 2), bf16),
        ],
        grad_sources + [hidden, grad_second],
        work * (WIDE + rank),
    )
    kept_in = call(
        functools.partial(grad_in_kernel, loss_scale),
        pairs,
        source_specs + [unit_spec, whole_rank],
        [tile_in, tile_in, low_in, low_in],
        [
            sds(tile_in_dims, f32),
            sds(tile_in_dims, bf16),
            sds((rank // 2, units), f32),
            sds((rank // 2, units), bf16),
        ],
        token_sources + [pre_grad, low_first],
        work * (WIDE + rank),
    )

    def tok_sum(keep, send):
        return keep + partner(send, "tok", 1).astype(f32)

    def tok_halves(value, axis):
        low, high = jnp.split(value, 2, axis=axis)
        second = lax.axis_index("tok") == 1
        return tok_sum(
            jnp.where(second, high, low), jnp.where(second, low, high).astype(bf16)
        )

    grad_low_out_b = tok_halves(dot(low_second, residual_grad, 0, 0) * loss_scale, 0)
    grad_bfly_out = tok_sum(kept_out[0], kept_out[1])
    grad_low_out_a = tok_sum(kept_out[2], kept_out[3])
    grad_bfly_in = tok_sum(kept_in[0], kept_in[1])
    grad_low_in_b = tok_sum(kept_in[2], kept_in[3])
    grad_low_in_a = tok_halves(dot(tokens, grad_first, 0, 0) * loss_scale, 1)
    feat = feat_total + dot(grad_first, low_in_a, 1, 1)
    for arrived in feat_arrived:
        feat = feat + arrived.astype(f32)
    grad_tokens = feat.astype(bf16)
    return (
        student,
        grad_tokens,
        grad_bfly_in,
        grad_bfly_out,
        grad_low_in_a,
        grad_low_in_b,
        grad_low_out_a,
        grad_low_out_b,
    )


def solution(mesh):
    placed = (
        P(("pop", "tok"), "hid"),
        P(("pop", "tok"), "hid"),
        P(("pop", "tok")),
        P(("pop", "hid"), None, None, None),
        P(("pop", "hid"), None, None, None),
        P(("pop", "hid"), None),
        P("pop", "hid"),
        P(("pop", "hid"), None),
        P("pop", "hid"),
        P("hid", None),
    )
    return jax.shard_map(
        on_device,
        mesh=mesh,
        in_specs=placed,
        out_specs=(
            P(("pop", "tok"), "hid"),
            P(("pop", "tok"), "hid"),
            P(("pop", "hid"), None, None, "tok"),
            P(("pop", "hid"), None, "tok", None),
            P(("pop", "hid"), "tok"),
            P(("pop", "tok"), "hid"),
            P(("pop", "hid"), "tok"),
            P(("pop", "tok"), "hid"),
        ),
        check_vma=False,
    )
```

time: 1220 us -> 573 us (0.47)
  blocking collectives: 487 us -> 0 us
  matrix products: 403 us -> 9.32 us
  waiting for transfers between devices: 0.14 us -> 293 us
  local copies, waits for them, and re-layouts: 261 us -> 45.8 us
  Pallas kernels: 0 us -> 108 us
  other arithmetic: 26 us -> 74.1 us
  starting transfers between devices: 19.2 us -> 40.9 us
  between operations: 14.9 us -> 1.4 us
    psum x4 -> x0, blocking collectives: 487 us -> none  [rank_sum(): return lax.psum(term(), 'hid').astype(jnp.bfloat16)]
    dot_general x60 -> x6, matrix products: 403 us -> 9.32 us  [dot(): lax.dot_general(left, right, (((left_dim,), (right_dim,)), ((), ())), pre...]
    ppermute x12 -> x42, waiting for transfers between devices: 0.03 us -> 293 us  [partner(): return lax.ppermute(value, axis, pairs)]
    gather x18 -> x0, local copies, waits for them, and re-layouts: 203 us -> none  [the longest x1 76.1 us: on_device(): jnp.take_along_axis(activated, hidden_order[None], axis=2)]
    pallas_call x0 -> x4, Pallas kernels: none -> 108 us  [call(): pl.pallas_call(kernel, grid=(pairs,), in_specs=in_specs, out_specs=out_sp...]
    reshape x4 -> x1, local copies, waits for them, and re-layouts: 32.5 us -> 0.01 us  [on_device(): order = hidden_order.reshape(pairs, 2, BLK)]
    add x0 -> x14, other arithmetic: none -> 30.7 us  [the longest x6 26.2 us: tok_sum(): return keep + partner(send, 'tok', 1).astype(f32)]
    concatenate x0 -> x14, other arithmetic: none -> 23.1 us  [the longest x2 12.3 us: pair_weights(): jnp.concatenate([pairs[:, :, :1], jnp.zeros_like(pairs[:, :, 1:LEVELS])],...]
  transfers between devices with their start and end apart: 18 -> 42, of which waited for: 0 -> 21; matrix products, arithmetic and copies ran while one was open for 29% -> 19% of each run, Pallas kernels for 0% -> 6%
where the time goes in v1:
time: 573 us; the launch traced here: 572 us
  waiting for transfers between devices  293 us (51%)
  Pallas kernels  108 us (19%)
  other arithmetic  74.1 us (13%)
  local copies, waits for them, and re-layouts  45.8 us (8%)
  starting transfers between devices  40.9 us (7%)
  matrix products  9.32 us (2%)
    ppermute x42, waiting for transfers between devices, partner(): return lax.ppermute(value, axis, pairs)  293 us
    pallas_call x4, Pallas kernels, call(): pl.pallas_call(kernel, grid=(pairs,), in_specs=in_specs, out_specs=out_sp...  108 us
    ppermute x42, starting transfers between devices, partner(): return lax.ppermute(value, axis, pairs)  40.9 us
    unnamed x59, local copies, waits for them, and re-layouts  26.4 us
    add x6, other arithmetic, tok_sum(): return keep + partner(send, 'tok', 1).astype(f32)  26.2 us
    concatenate x2, other arithmetic, pair_weights(): jnp.concatenate([pairs[:, :, :1], jnp.zeros_like(pairs[:, :, 1:LEVELS])],...  12.3 us
  transfers between devices with their start and end apart: 42, of which 21 were waited for; matrix products, arithmetic and copies ran while one was open for 19% of the time, Pallas kernels for 6%

profile of v1, /device:TPU:0, one launch (start us, length us, event | category | flops | bytes accessed | tf_op | source)
XLA Modules:
  0.0 572.2 jit_solution(5442771648330944192)
XLA Ops:
  0.6 3.0 collective-permute-start
  5.2 2.6 collective-permute-start.2
  7.8 2.7 fusion.12
  11.2 5.5 copy_select_fusion
  19.6 2.5 slice_bitcast_fusion.3
  22.2 24.6 %collective-permute-done.3 = bf16[384,512]{1,0:T(8,128)(2,1)} collective-permute-done((bf16[384,512]{1,0:T(8,128)(2,1)S(1)}, bf16[384,512]{1,0:T(8,128)(2,1)}, u32[]{:S(2)}, u32[]{:S(2)}) %collective-permute-start.3) | collective-permute-done | bytes 393248 | tf_op jit(solution)/shard_map/ppermute | solution.py:26
  50.2 27.4 %collective-permute-done.4 = bf16[192,512]{1,0:T(8,128)(2,1)S(1)} collective-permute-done((bf16[192,512]{1,0:T(8,128)(2,1)S(1)}, bf16[192,512]{1,0:T(8,128)(2,1)S(1)}, u32[]{:S(2)}, u32[]{:S(2)}) %collective-permute-start.4) | collective-permute-done | bytes 196640 | tf_op jit(solution)/shard_map/ppermute | solution.py:26
  77.8 2.7 collective-permute-start.5
  80.5 3.8 maximum_maximum_fusion
  87.5 7.8 %copy.46 = bf16[8,2,7,256,64]{4,3,2,0,1:T(8,128)(2,1)} copy(bf16[8,2,7,256,64]{3,4,2,1,0:T(8,128)(2,1)} %slice.69) | data formatting | bytes 7340032
  95.7 6.8 %broadcast_select_fusion = bf16[8,2,7,256,64]{4,3,2,0,1:T(8,128)(2,1)} fusion(bf16[8,2,7,256,64]{4,3,2,0,1:T(8,128)(2,1)} %copy.46, pred[7]{0:T(512)(128)(4,1)S(1)} %copy-done.19), kind=kLoop, calls=%fused_computation.5 | loop fusion | flops 1835008 | bytes 7340039 | tf_op jit(solution)/shard_map/concatenate | solution.py:58
  105.1 6.8 %copy.45 = bf16[8,2,6,256,64]{4,3,2,0,1:T(8,128)(2,1)} copy(bf16[8,2,6,256,64]{3,4,2,1,0:T(8,128)(2,1)} %slice.66) | data formatting | bytes 6291456
  113.7 5.7 fusion.1
  120.1 6.0 %maximum_maximum_fusion.1.refs_8_ = bf16[8,7,512,128]{3,2,1,0:T(8,128)(2,1)} fusion(bf16[8,7,256,64]{3,2,1,0:T(8,128)(2,1)S(1)} %get-tuple-element.77, bf16[8,7,256,64]{3,2,1,0:T(8,128)(2,1)S(1)} %get-tuple-element.108, bf16[8,7,256,64]{3,2,1,0:T(8,128)(2,1)S(1)} %get-tuple-element.109, bf16[8,7,256,64]{3,2,1,0:T(8,128)(2,1)S(1)} %get-tuple-element.76), kind=kLoop, calls=%fused_computation.4 | loop fusion | flops 29360128 | bytes 14680064 | tf_op jit(solution)/shard_map/concatenate | solution.py:74
  126.1 2.3 collective-permute-done.8
  128.7 38.9 %shard_map.161 = (bf16[768,4096]{1,0:T(8,128)(2,1)}, bf16[768,4096]{1,0:T(8,128)(2,1)}, f32[768,1024]{1,0:T(8,128)}, f32[768,512]{1,0:T(8,128)}, bf16[768,1024]{...) custom-call(bf16[768,1024]{1,0:T(8,128)(2,1)} %refs_3_.3, bf16[768,1024]{1,0:T(8,128)(2,1)} %refs_3_.3, ...), custom_call_target="tpu_custom_call" | custom-call | flops 20937965568 | bytes 56901632 | tf_op jit(solution)/shard_map/pallas_call | solution.py:204
  169.8 7.5 %collective-permute-done.9 = bf16[384,512]{1,0:T(8,128)(2,1)S(1)} collective-permute-done((bf16[384,512]{1,0:T(8,128)(2,1)S(1)}, bf16[384,512]{1,0:T(8,128)(2,1)S(1)}, u32[]{:S(2)}, u32[]{:S(2)}) %collective-permute-start.9) | collective-permute-done | bytes 393248 | tf_op jit(solution)/shard_map/ppermute | solution.py:26
  179.3 6.5 %collective-permute-done.10 = bf16[192,512]{1,0:T(8,128)(2,1)S(1)} collective-permute-done((bf16[192,512]{1,0:T(8,128)(2,1)S(1)}, bf16[192,512]{1,0:T(8,128)(2,1)S(1)}, u32[]{:S(2)}, u32[]{:S(2)}) %collective-permute-start.10) | collective-permute-done | bytes 196640 | tf_op jit(solution)/shard_map/ppermute | solution.py:26
  187.5 22.3 %collective-permute-done.11 = bf16[96,512]{1,0:T(8,128)(2,1)S(1)} collective-permute-done((bf16[96,512]{1,0:T(8,128)(2,1)S(1)}, bf16[96,512]{1,0:T(8,128)(2,1)S(1)}, u32[]{:S(2)}, u32[]{:S(2)}) %collective-permute-start.11) | collective-permute-done | bytes 98336 | tf_op jit(solution)/shard_map/ppermute | solution.py:26
  210.0 2.9 collective-permute-start.17
  214.2 3.7 collective-permute-done.12
  218.0 46.6 %collective-permute-done.13 = bf16[192,512]{1,0:T(8,128)(2,1)S(1)} collective-permute-done((bf16[192,512]{1,0:T(8,128)(2,1)S(1)}, bf16[192,512]{1,0:T(8,128)(2,1)S(1)}, u32[]{:S(2)}, u32[]{:S(2)}) %collective-permute-start.13) | collective-permute-done | bytes 196640 | tf_op jit(solution)/shard_map/ppermute | solution.py:26
  265.8 6.8 %collective-permute-done.14 = bf16[384,512]{1,0:T(8,128)(2,1)S(1)} collective-permute-done((bf16[384,512]{1,0:T(8,128)(2,1)S(1)}, bf16[384,512]{1,0:T(8,128)(2,1)S(1)}, u32[]{:S(2)}, u32[]{:S(2)}) %collective-permute-start.14) | collective-permute-done | bytes 393248 | tf_op jit(solution)/shard_map/ppermute | solution.py:26
  273.8 3.3 multiply_convert_fusion
  279.2 11.1 %collective-permute-done.21 = bf16[384,512]{1,0:T(8,128)(2,1)S(1)} collective-permute-done((bf16[384,512]{1,0:T(8,128)(2,1)S(1)}, bf16[384,512]{1,0:T(8,128)(2,1)S(1)}, u32[]{:S(2)}, u32[]{:S(2)}) %collective-permute-start.21) | collective-permute-done | bytes 393248 | tf_op jit(solution)/shard_map/ppermute | solution.py:26
  290.6 14.2 %collective-permute-done.22 = bf16[192,512]{1,0:T(8,128)(2,1)S(1)} collective-permute-done((bf16[192,512]{1,0:T(8,128)(2,1)S(1)}, bf16[192,512]{1,0:T(8,128)(2,1)S(1)}, u32[]{:S(2)}, u32[]{:S(2)}) %collective-permute-start.22) | collective-permute-done | bytes 196640 | tf_op jit(solution)/shard_map/ppermute | solution.py:26
  305.0 15.5 %collective-permute-done.23 = bf16[96,512]{1,0:T(8,128)(2,1)S(1)} collective-permute-done((bf16[96,512]{1,0:T(8,128)(2,1)S(1)}, bf16[96,512]{1,0:T(8,128)(2,1)S(1)}, u32[]{:S(2)}, u32[]{:S(2)}) %collective-permute-start.23) | collective-permute-done | bytes 98336 | tf_op jit(solution)/shard_map/ppermute | solution.py:26
  321.5 3.2 collective-permute-start.19
  326.7 34.9 %collective-permute-done.25 = bf16[192,512]{1,0:T(8,128)(2,1)S(1)} collective-permute-done((bf16[192,512]{1,0:T(8,128)(2,1)S(1)}, bf16[192,512]{1,0:T(8,128)(2,1)S(1)}, u32[]{:S(2)}, u32[]{:S(2)}) %collective-permute-start.25) | collective-permute-done | bytes 196640 | tf_op jit(solution)/shard_map/ppermute | solution.py:26
  362.6 7.0 %collective-permute-done.26 = bf16[384,512]{1,0:T(8,128)(2,1)S(1)} collective-permute-done((bf16[384,512]{1,0:T(8,128)(2,1)S(1)}, bf16[384,512]{1,0:T(8,128)(2,1)S(1)}, u32[]{:S(2)}, u32[]{:S(2)}) %collective-permute-start.26) | collective-permute-done | bytes 393248 | tf_op jit(solution)/shard_map/ppermute | solution.py:26
  372.0 35.1 %shard_map.162 = (bf16[768,4096]{1,0:T(8,128)(2,1)}, f32[768,1024]{1,0:T(8,128)}, f32[768,512]{1,0:T(8,128)}, bf16[768,1024]{1,0:T(8,128)(2,1)}, bf16[768,1024]{1,0:T(8,128)(2,1)}, /*index=5*/bf16[768,1024]{1,0:T(8,128)(2,1)}) custom-call(bf16[768,1024]{1,0:T(8,128)(2,1)} %copy-done.13, bf16[768,1024]{1,0:T(8,128)(2,1)} %copy-done.13, ...), custom_call_target="tpu_custom_call" | custom-call | flops 19327352832 | bytes 56901632 | tf_op jit(solution)/shard_map/pallas_call | solution.py:204
  410.2 2.7 convolution_multiply_fusion
  412.8 4.6 collective-permute-done.27
  418.7 2.5 collective-permute-start.28
  421.4 4.1 collective-permute-done.28
  427.8 23.0 %collective-permute-done.29 = bf16[96,512]{1,0:T(8,128)(2,1)S(1)} collective-permute-done((bf16[96,512]{1,0:T(8,128)(2,1)S(1)}, bf16[96,512]{1,0:T(8,128)(2,1)S(1)}, u32[]{:S(2)}, u32[]{:S(2)}) %collective-permute-start.29) | collective-permute-done | bytes 98336 | tf_op jit(solution)/shard_map/ppermute | solution.py:26
  452.1 2.9 collective-permute-start.35
  459.2 17.7 %shard_map.164 = (f32[16,8,128,64]{3,2,1,0:T(8,128)}, bf16[16,8,128,64]{3,2,1,0:T(8,128)(2,1)}, f32[4096,256]{1,0:T(8,128)}, bf16[4096,256]{1,0:T(8,128)(2,1)}) custom-call(bf16[768,1024]{1,0:T(8,128)(2,1)} %copy-done.13, bf16[768,1024]{1,0:T(8,128)(2,1)} %copy-done.13, bf16[768,1024]{1,0:T(8,128)(2,1)} %copy-done.13, bf16[768,1024]{1,0:T(8,128)(2,1)} %copy-done.13, ...), custom_call_target="tpu_custom_call" | custom-call | flops 8858370048 | bytes 30670848 | tf_op jit(solution)/shard_map/pallas_call | solution.py:204
  476.9 4.8 copy.37
  481.7 26.1 %collective-permute-done.31 = bf16[192,512]{1,0:T(8,128)(2,1)} collective-permute-done((bf16[192,512]{1,0:T(8,128)(2,1)}, bf16[192,512]{1,0:T(8,128)(2,1)}, u32[]{:S(2)}, u32[]{:S(2)}) %collective-permute-start.31) | collective-permute-done | bytes 196640 | tf_op jit(solution)/shard_map/ppermute | solution.py:26
  509.3 16.3 %shard_map.163 = (f32[16,8,64,128]{3,2,1,0:T(8,128)}, bf16[16,8,64,128]{3,2,1,0:T(8,128)(2,1)}, f32[256,4096]{1,0:T(8,128)}, bf16[256,4096]{1,0:T(8,128)(2,1)}) custom-call(bf16[768,1024]{1,0:T(8,128)(2,1)} %refs_3_.3, bf16[768,1024]{1,0:T(8,128)(2,1)} %refs_3_.3, bf16[768,1024]{1,0:T(8,128)(2,1)} %refs_3_.3, bf16[768,1024]{1,0:T(8,128)(2,1)} %refs_3_.3, ...), custom_call_target="tpu_custom_call" | custom-call | flops 8858370048 | bytes 30670848 | tf_op jit(solution)/shard_map/pallas_call | solution.py:204
  529.2 4.6 add_convert_fusion
  535.9 4.8 copy.38
  540.6 10.0 %convert_add_fusion = f32[16,8,128,64]{3,2,1,0:T(8,128)} fusion(f32[16,8,128,64]{3,2,1,0:T(8,128)} %get-tuple-element.44, bf16[16,8,128,64]{3,2,1,0:T(8,128)(2,1)} %copy.38), kind=kLoop, calls=%fused_computation | loop fusion | flops 2097152 | bytes 10485760 | tf_op jit(solution)/shard_map/add | solution.py:346
  550.6 6.8 %copy.39 = f32[16,8,128,64]{2,3,1,0:T(8,128)} copy(f32[16,8,128,64]{3,2,1,0:T(8,128)} %convert_add_fusion) | data formatting | bytes 8388608
  557.4 6.1 %convert_add_fusion.3 = f32[16,8,64,128]{3,2,1,0:T(8,128)} fusion(f32[16,8,64,128]{3,2,1,0:T(8,128)} %get-tuple-element.41, bf16[16,8,64,128]{3,2,1,0:T(8,128)(2,1)} %collective-permute-done.36), kind=kLoop, calls=%fused_computation.8 | loop fusion | flops 2097152 | bytes 10485760 | tf_op jit(solution)/shard_map/add | solution.py:346
  563.5 4.4 convert_add_fusion.2
  567.9 4.2 convert_add_fusion.1
  (177 shorter events, 55.7 us)
Async XLA Ops:
  0.6 272.1 %copy-start = (bf16[512,1024]{1,0:T(8,128)(2,1)S(1)}, bf16[512,1024]{1,0:T(8,128)(2,1)}, u32[]{:S(2)}) copy-start(bf16[512,1024]{1,0:T(8,128)(2,1)} %param.18) | copy-start | bytes 3145732
  0.6 128.0 %collective-permute-start = (bf16[768,1024]{1,0:T(8,128)(2,1)}, bf16[768,1024]{1,0:T(8,128)(2,1)}, u32[]{:S(2)}, u32[]{:S(2)}) collective-permute-start(bf16[768,1024]{1,0:T(8,128)(2,1)} %refs_3_.3), channel_id=1, source_target_pairs={{0,2},{2,0},{4,6},{6,4},{8,10},{10,8},{12,14},{14,12},{1,3},{3,1},... | collective-permute-start | bytes 4718600 | tf_op jit(solution)/shard_map/ppermute | solution.py:26
  3.7 125.0 %collective-permute-start.1 = (bf16[768,1024]{1,0:T(8,128)(2,1)}, bf16[768,1024]{1,0:T(8,128)(2,1)}, u32[]{:S(2)}, u32[]{:S(2)}) collective-permute-start(bf16[768,1024]{1,0:T(8,128)(2,1)} %refs_3_.3), channel_id=1, source_target_pairs={{0,4},{2,6},{4,0},{6,2},{8,12},{10,14},{12,8},{14,10},{1,5},{3,7},... | collective-permute-start | bytes 4718600 | tf_op jit(solution)/shard_map/ppermute | solution.py:26
  5.2 123.5 %collective-permute-start.2 = (bf16[768,1024]{1,0:T(8,128)(2,1)}, bf16[768,1024]{1,0:T(8,128)(2,1)}, u32[]{:S(2)}, u32[]{:S(2)}) collective-permute-start(bf16[768,1024]{1,0:T(8,128)(2,1)} %refs_3_.3), channel_id=1, source_target_pairs={{0,8},{2,10},{4,12},{6,14},{8,0},{10,2},{12,4},{14,6},{1,9},{3,11}... | collective-permute-start | bytes 4718600 | tf_op jit(solution)/shard_map/ppermute | solution.py:26
  10.6 36.2 %collective-permute-start.3 = (bf16[384,512]{1,0:T(8,128)(2,1)S(1)}, bf16[384,512]{1,0:T(8,128)(2,1)}, u32[]{:S(2)}, u32[]{:S(2)}) collective-permute-start(bf16[384,512]{1,0:T(8,128)(2,1)S(1)} %select_convert_fusion.5), channel_id=1, source_target_pairs={{0,2},{2,0},{4,6},{6,4},{8,10},{10,8},{12,14},{14,12},{1,3},{3,1},... | collective-permute-start | bytes 1179656 | tf_op jit(solution)/shard_map/ppermute | solution.py:26
  48.0 29.6 %collective-permute-start.4 = (bf16[192,512]{1,0:T(8,128)(2,1)S(1)}, bf16[192,512]{1,0:T(8,128)(2,1)S(1)}, u32[]{:S(2)}, u32[]{:S(2)}) collective-permute-start(bf16[192,512]{1,0:T(8,128)(2,1)S(1)} %select_convert_fusion.9), channel_id=1, source_target_pairs={{0,4},{2,6},{4,0},{6,2},{8,12},{10,14},{12,8},{14,10},{1,5},{3,7},... | collective-permute-start | bytes 589832 | tf_op jit(solution)/shard_map/ppermute | solution.py:26
  77.8 17.6 %collective-permute-start.5 = (bf16[96,512]{1,0:T(8,128)(2,1)S(1)}, bf16[96,512]{1,0:T(8,128)(2,1)S(1)}, u32[]{:S(2)}, u32[]{:S(2)}) collective-permute-start(bf16[96,512]{1,0:T(8,128)(2,1)S(1)} %select_convert_fusion.13), channel_id=1, source_target_pairs={{0,8},{2,10},{4,12},{6,14},{8,0},{10,2},{12,4},{14,6},{1,9},{3,11}... | collective-permute-start | bytes 294920 | tf_op jit(solution)/shard_map/ppermute | solution.py:26
  95.4 16.5 %collective-permute-start.6 = (bf16[96,512]{1,0:T(8,128)(2,1)S(1)}, bf16[96,512]{1,0:T(8,128)(2,1)S(1)}, u32[]{:S(2)}, u32[]{:S(2)}) collective-permute-start(bf16[96,512]{1,0:T(8,128)(2,1)S(1)} %add_convert_fusion.5), channel_id=1, source_target_pairs={{0,8},{2,10},{4,12},{6,14},{8,0},{10,2},{12,4},{14,6},{1,9},{3,11}... | collective-permute-start | bytes 294920 | tf_op jit(solution)/shard_map/ppermute | solution.py:26
  112.0 7.4 %collective-permute-start.7 = (bf16[192,512]{1,0:T(8,128)(2,1)S(1)}, bf16[192,512]{1,0:T(8,128)(2,1)S(1)}, u32[]{:S(2)}, u32[]{:S(2)}) collective-permute-start(bf16[192,512]{1,0:T(8,128)(2,1)S(1)} %pad_maximum_fusion.14), channel_id=1, source_target_pairs={{0,4},{2,6},{4,0},{6,2},{8,12},{10,14},{12,8},{14,10},{1,5},{3,7},... | collective-permute-start | bytes 589832 | tf_op jit(solution)/shard_map/ppermute | solution.py:26
  119.5 9.0 %collective-permute-start.8 = (bf16[384,512]{1,0:T(8,128)(2,1)S(1)}, bf16[384,512]{1,0:T(8,128)(2,1)S(1)}, u32[]{:S(2)}, u32[]{:S(2)}) collective-permute-start(bf16[384,512]{1,0:T(8,128)(2,1)S(1)} %pad_maximum_fusion.10), channel_id=1, source_target_pairs={{0,2},{2,0},{4,6},{6,4},{8,10},{10,8},{12,14},{14,12},{1,3},{3,1},... | collective-permute-start | bytes 1179656 | tf_op jit(solution)/shard_map/ppermute | solution.py:26
  167.6 42.3 %copy-start.26 = (bf16[768,1024]{1,0:T(8,128)(2,1)S(1)}, bf16[768,1024]{1,0:T(8,128)(2,1)}, u32[]{:S(2)}) copy-start(bf16[768,1024]{1,0:T(8,128)(2,1)} %get-tuple-element.33) | copy-start | bytes 4718596
  167.6 45.2 %copy-start.25 = (bf16[768,1024]{1,0:T(8,128)(2,1)S(1)}, bf16[768,1024]{1,0:T(8,128)(2,1)}, u32[]{:S(2)}) copy-start(bf16[768,1024]{1,0:T(8,128)(2,1)} %get-tuple-element.32) | copy-start | bytes 4718596
  167.6 45.9 %copy-start.24 = (bf16[768,1024]{1,0:T(8,128)(2,1)S(1)}, bf16[768,1024]{1,0:T(8,128)(2,1)}, u32[]{:S(2)}) copy-start(bf16[768,1024]{1,0:T(8,128)(2,1)} %get-tuple-element.31) | copy-start | bytes 4718596
  169.2 8.1 %collective-permute-start.9 = (bf16[384,512]{1,0:T(8,128)(2,1)S(1)}, bf16[384,512]{1,0:T(8,128)(2,1)S(1)}, u32[]{:S(2)}, u32[]{:S(2)}) collective-permute-start(bf16[384,512]{1,0:T(8,128)(2,1)S(1)} %select_convert_fusion.4), channel_id=1, source_target_pairs={{0,2},{2,0},{4,6},{6,4},{8,10},{10,8},{12,14},{14,12},{1,3},{3,1},... | collective-permute-start | bytes 1179656 | tf_op jit(solution)/shard_map/ppermute | solution.py:26
  178.9 86.9 %copy-start.18 = (s32[768]{0:T(1024)S(1)}, s32[768]{0:T(1024)}, u32[]{:S(2)}) copy-start(s32[768]{0:T(1024)} %param.12) | copy-start | bytes 9220
  178.9 6.8 %collective-permute-start.10 = (bf16[192,512]{1,0:T(8,128)(2,1)S(1)}, bf16[192,512]{1,0:T(8,128)(2,1)S(1)}, u32[]{:S(2)}, u32[]{:S(2)}) collective-permute-start(bf16[192,512]{1,0:T(8,128)(2,1)S(1)} %select_convert_fusion.8), channel_id=1, source_target_pairs={{0,4},{2,6},{4,0},{6,2},{8,12},{10,14},{12,8},{14,10},{1,5},{3,7},... | collective-permute-start | bytes 589832 | tf_op jit(solution)/shard_map/ppermute | solution.py:26
  185.8 24.0 %collective-permute-start.11 = (bf16[96,512]{1,0:T(8,128)(2,1)S(1)}, bf16[96,512]{1,0:T(8,128)(2,1)S(1)}, u32[]{:S(2)}, u32[]{:S(2)}) collective-permute-start(bf16[96,512]{1,0:T(8,128)(2,1)S(1)} %select_convert_fusion.12), channel_id=1, source_target_pairs={{0,8},{2,10},{4,12},{6,14},{8,0},{10,2},{12,4},{14,6},{1,9},{3,11}... | collective-permute-start | bytes 294920 | tf_op jit(solution)/shard_map/ppermute | solution.py:26
  209.9 8.0 %collective-permute-start.12 = (bf16[96,512]{1,0:T(8,128)(2,1)S(1)}, bf16[96,512]{1,0:T(8,128)(2,1)S(1)}, u32[]{:S(2)}, u32[]{:S(2)}) collective-permute-start(bf16[96,512]{1,0:T(8,128)(2,1)S(1)} %add_convert_fusion.4), channel_id=1, source_target_pairs={{0,8},{2,10},{4,12},{6,14},{8,0},{10,2},{12,4},{14,6},{1,9},{3,11}... | collective-permute-start | bytes 294920 | tf_op jit(solution)/shard_map/ppermute | solution.py:26
  210.0 63.7 %collective-permute-start.17 = (bf16[768,1024]{1,0:T(8,128)(2,1)S(1)}, bf16[768,1024]{1,0:T(8,128)(2,1)S(1)}, u32[]{:S(2)}, u32[]{:S(2)}) collective-permute-start(bf16[768,1024]{1,0:T(8,128)(2,1)S(1)} %copy-done.26), channel_id=1, source_target_pairs={{0,8},{2,10},{4,12},{6,14},{8,0},{10,2},{12,4},{14,6},{1,9},{3,11}... | collective-permute-start | bytes 4718600 | tf_op jit(solution)/shard_map/ppermute | solution.py:26
  212.9 60.9 %collective-permute-start.16 = (bf16[768,1024]{1,0:T(8,128)(2,1)S(1)}, bf16[768,1024]{1,0:T(8,128)(2,1)S(1)}, u32[]{:S(2)}, u32[]{:S(2)}) collective-permute-start(bf16[768,1024]{1,0:T(8,128)(2,1)S(1)} %copy-done.25), channel_id=1, source_target_pairs={{0,4},{2,6},{4,0},{6,2},{8,12},{10,14},{12,8},{14,10},{1,5},{3,7},... | collective-permute-start | bytes 4718600 | tf_op jit(solution)/shard_map/ppermute | solution.py:26
  213.5 60.2 %collective-permute-start.15 = (bf16[768,1024]{1,0:T(8,128)(2,1)S(1)}, bf16[768,1024]{1,0:T(8,128)(2,1)S(1)}, u32[]{:S(2)}, u32[]{:S(2)}) collective-permute-start(bf16[768,1024]{1,0:T(8,128)(2,1)S(1)} %copy-done.24), channel_id=1, source_target_pairs={{0,2},{2,0},{4,6},{6,4},{8,10},{10,8},{12,14},{14,12},{1,3},{3,1},... | collective-permute-start | bytes 4718600 | tf_op jit(solution)/shard_map/ppermute | solution.py:26
  217.9 46.7 %collective-permute-start.13 = (bf16[192,512]{1,0:T(8,128)(2,1)S(1)}, bf16[192,512]{1,0:T(8,128)(2,1)S(1)}, u32[]{:S(2)}, u32[]{:S(2)}) collective-permute-start(bf16[192,512]{1,0:T(8,128)(2,1)S(1)} %pad_maximum_fusion.15), channel_id=1, source_target_pairs={{0,4},{2,6},{4,0},{6,2},{8,12},{10,14},{12,8},{14,10},{1,5},{3,7},... | collective-permute-start | bytes 589832 | tf_op jit(solution)/shard_map/ppermute | solution.py:26
  264.7 7.8 %collective-permute-start.14 = (bf16[384,512]{1,0:T(8,128)(2,1)S(1)}, bf16[384,512]{1,0:T(8,128)(2,1)S(1)}, u32[]{:S(2)}, u32[]{:S(2)}) collective-permute-start(bf16[384,512]{1,0:T(8,128)(2,1)S(1)} %pad_maximum_fusion.11), channel_id=1, source_target_pairs={{0,2},{2,0},{4,6},{6,4},{8,10},{10,8},{12,14},{14,12},{1,3},{3,1},... | collective-permute-start | bytes 1179656 | tf_op jit(solution)/shard_map/ppermute | solution.py:26
  277.1 47.6 %copy-start.13 = (bf16[768,1024]{1,0:T(8,128)(2,1)}, bf16[768,1024]{1,0:T(8,128)(2,1)S(1)}, u32[]{:S(2)}) copy-start(bf16[768,1024]{1,0:T(8,128)(2,1)S(1)} %get-tuple-element.74.refs_0_.refs_1_.refs_2_.refs_3_) | copy-start | bytes 4718596
  278.1 12.1 %collective-permute-start.21 = (bf16[384,512]{1,0:T(8,128)(2,1)S(1)}, bf16[384,512]{1,0:T(8,128)(2,1)S(1)}, u32[]{:S(2)}, u32[]{:S(2)}) collective-permute-start(bf16[384,512]{1,0:T(8,128)(2,1)S(1)} %select_convert_fusion.3), channel_id=1, source_target_pairs={{0,2},{2,0},{4,6},{6,4},{8,10},{10,8},{12,14},{14,12},{1,3},{3,1},... | collective-permute-start | bytes 1179656 | tf_op jit(solution)/shard_map/ppermute | solution.py:26
  290.5 14.3 %collective-permute-start.22 = (bf16[192,512]{1,0:T(8,128)(2,1)S(1)}, bf16[192,512]{1,0:T(8,128)(2,1)S(1)}, u32[]{:S(2)}, u32[]{:S(2)}) collective-permute-start(bf16[192,512]{1,0:T(8,128)(2,1)S(1)} %select_convert_fusion.7), channel_id=1, source_target_pairs={{0,4},{2,6},{4,0},{6,2},{8,12},{10,14},{12,8},{14,10},{1,5},{3,7},... | collective-permute-start | bytes 589832 | tf_op jit(solution)/shard_map/ppermute | solution.py:26
  305.0 15.6 %collective-permute-start.23 = (bf16[96,512]{1,0:T(8,128)(2,1)S(1)}, bf16[96,512]{1,0:T(8,128)(2,1)S(1)}, u32[]{:S(2)}, u32[]{:S(2)}) collective-permute-start(bf16[96,512]{1,0:T(8,128)(2,1)S(1)} %select_convert_fusion.11), channel_id=1, source_target_pairs={{0,8},{2,10},{4,12},{6,14},{8,0},{10,2},{12,4},{14,6},{1,9},{3,11}... | collective-permute-start | bytes 294920 | tf_op jit(solution)/shard_map/ppermute | solution.py:26
  320.6 6.0 %collective-permute-start.24 = (bf16[96,512]{1,0:T(8,128)(2,1)S(1)}, bf16[96,512]{1,0:T(8,128)(2,1)S(1)}, u32[]{:S(2)}, u32[]{:S(2)}) collective-permute-start(bf16[96,512]{1,0:T(8,128)(2,1)S(1)} %add_convert_fusion.3), channel_id=1, source_target_pairs={{0,8},{2,10},{4,12},{6,14},{8,0},{10,2},{12,4},{14,6},{1,9},{3,11}... | collective-permute-start | bytes 294920 | tf_op jit(solution)/shard_map/ppermute | solution.py:26
  320.7 49.1 %collective-permute-start.18 = (bf16[768,1024]{1,0:T(8,128)(2,1)S(1)}, bf16[768,1024]{1,0:T(8,128)(2,1)S(1)}, u32[]{:S(2)}, u32[]{:S(2)}) collective-permute-start(bf16[768,1024]{1,0:T(8,128)(2,1)S(1)} %get-tuple-element.74.refs_0_.refs_1_.refs_2_.refs_3_), channel_id=1, source_target_pairs={{0,2},{2,0},{4,6},{6,4},{8,10},{10,8},{12,14},{14,12},{1,3},{3,1},... | collective-permute-start | bytes 4718600 | tf_op jit(solution)/shard_map/ppermute | solution.py:26
  321.5 48.3 %collective-permute-start.19 = (bf16[768,1024]{1,0:T(8,128)(2,1)S(1)}, bf16[768,1024]{1,0:T(8,128)(2,1)S(1)}, u32[]{:S(2)}, u32[]{:S(2)}) collective-permute-start(bf16[768,1024]{1,0:T(8,128)(2,1)S(1)} %get-tuple-element.74.refs_0_.refs_1_.refs_2_.refs_3_), channel_id=1, source_target_pairs={{0,4},{2,6},{4,0},{6,2},{8,12},{10,14},{12,8},{14,10},{1,5},{3,7},... | collective-permute-start | bytes 4718600 | tf_op jit(solution)/shard_map/ppermute | solution.py:26
  324.7 45.1 %collective-permute-start.20 = (bf16[768,1024]{1,0:T(8,128)(2,1)S(1)}, bf16[768,1024]{1,0:T(8,128)(2,1)S(1)}, u32[]{:S(2)}, u32[]{:S(2)}) collective-permute-start(bf16[768,1024]{1,0:T(8,128)(2,1)S(1)} %get-tuple-element.74.refs_0_.refs_1_.refs_2_.refs_3_), channel_id=1, source_target_pairs={{0,8},{2,10},{4,12},{6,14},{8,0},{10,2},{12,4},{14,6},{1,9},{3,11}... | collective-permute-start | bytes 4718600 | tf_op jit(solution)/shard_map/ppermute | solution.py:26
  326.6 35.0 %collective-permute-start.25 = (bf16[192,512]{1,0:T(8,128)(2,1)S(1)}, bf16[192,512]{1,0:T(8,128)(2,1)S(1)}, u32[]{:S(2)}, u32[]{:S(2)}) collective-permute-start(bf16[192,512]{1,0:T(8,128)(2,1)S(1)} %pad_maximum_fusion.16), channel_id=1, source_target_pairs={{0,4},{2,6},{4,0},{6,2},{8,12},{10,14},{12,8},{14,10},{1,5},{3,7},... | collective-permute-start | bytes 589832 | tf_op jit(solution)/shard_map/ppermute | solution.py:26
  361.7 7.8 %collective-permute-start.26 = (bf16[384,512]{1,0:T(8,128)(2,1)S(1)}, bf16[384,512]{1,0:T(8,128)(2,1)S(1)}, u32[]{:S(2)}, u32[]{:S(2)}) collective-permute-start(bf16[384,512]{1,0:T(8,128)(2,1)S(1)} %pad_maximum_fusion.12), channel_id=1, source_target_pairs={{0,2},{2,0},{4,6},{6,4},{8,10},{10,8},{12,14},{14,12},{1,3},{3,1},... | collective-permute-start | bytes 1179656 | tf_op jit(solution)/shard_map/ppermute | solution.py:26
  409.4 8.1 %collective-permute-start.27 = (bf16[384,512]{1,0:T(8,128)(2,1)}, bf16[384,512]{1,0:T(8,128)(2,1)}, u32[]{:S(2)}, u32[]{:S(2)}) collective-permute-start(bf16[384,512]{1,0:T(8,128)(2,1)} %select_convert_fusion.2), channel_id=1, source_target_pairs={{0,2},{2,0},{4,6},{6,4},{8,10},{10,8},{12,14},{14,12},{1,3},{3,1},... | collective-permute-start | bytes 1179656 | tf_op jit(solution)/shard_map/ppermute | solution.py:26
  418.7 6.8 %collective-permute-start.28 = (bf16[192,512]{1,0:T(8,128)(2,1)S(1)}, bf16[192,512]{1,0:T(8,128)(2,1)S(1)}, u32[]{:S(2)}, u32[]{:S(2)}) collective-permute-start(bf16[192,512]{1,0:T(8,128)(2,1)S(1)} %select_convert_fusion.6), channel_id=1, source_target_pairs={{0,4},{2,6},{4,0},{6,2},{8,12},{10,14},{12,8},{14,10},{1,5},{3,7},... | collective-permute-start | bytes 589832 | tf_op jit(solution)/shard_map/ppermute | solution.py:26
  421.3 29.5 %collective-permute-start.41 = (bf16[256,1024]{1,0:T(8,128)(2,1)S(1)}, bf16[256,1024]{1,0:T(8,128)(2,1)S(1)}, u32[]{:S(2)}, u32[]{:S(2)}) collective-permute-start(bf16[256,1024]{1,0:T(8,128)(2,1)S(1)} %select_convert_fusion), channel_id=1, source_target_pairs={{0,1},{1,0},{2,3},{3,2},{4,5},{5,4},{6,7},{7,6},{8,9},{9,8},{10,11... | collective-permute-start | bytes 1572872 | tf_op jit(solution)/shard_map/ppermute | solution.py:26
  425.6 25.2 %collective-permute-start.29 = (bf16[96,512]{1,0:T(8,128)(2,1)S(1)}, bf16[96,512]{1,0:T(8,128)(2,1)S(1)}, u32[]{:S(2)}, u32[]{:S(2)}) collective-permute-start(bf16[96,512]{1,0:T(8,128)(2,1)S(1)} %select_convert_fusion.10), channel_id=1, source_target_pairs={{0,8},{2,10},{4,12},{6,14},{8,0},{10,2},{12,4},{14,6},{1,9},{3,11}... | collective-permute-start | bytes 294920 | tf_op jit(solution)/shard_map/ppermute | solution.py:26
  450.8 7.7 %collective-permute-start.30 = (bf16[96,512]{1,0:T(8,128)(2,1)S(1)}, bf16[96,512]{1,0:T(8,128)(2,1)S(1)}, u32[]{:S(2)}, u32[]{:S(2)}) collective-permute-start(bf16[96,512]{1,0:T(8,128)(2,1)S(1)} %add_convert_fusion.2), channel_id=1, source_target_pairs={{0,8},{2,10},{4,12},{6,14},{8,0},{10,2},{12,4},{14,6},{1,9},{3,11}... | collective-permute-start | bytes 294920 | tf_op jit(solution)/shard_map/ppermute | solution.py:26
  452.1 76.0 %collective-permute-start.35 = (bf16[768,1024]{1,0:T(8,128)(2,1)}, bf16[768,1024]{1,0:T(8,128)(2,1)S(1)}, u32[]{:S(2)}, u32[]{:S(2)}) collective-permute-start(bf16[768,1024]{1,0:T(8,128)(2,1)} %get-tuple-element.39), channel_id=1, source_target_pairs={{0,8},{2,10},{4,12},{6,14},{8,0},{10,2},{12,4},{14,6},{1,9},{3,11}... | collective-permute-start | bytes 4718600 | tf_op jit(solution)/shard_map/ppermute | solution.py:26
  455.0 73.6 %collective-permute-start.34 = (bf16[768,1024]{1,0:T(8,128)(2,1)}, bf16[768,1024]{1,0:T(8,128)(2,1)}, u32[]{:S(2)}, u32[]{:S(2)}) collective-permute-start(bf16[768,1024]{1,0:T(8,128)(2,1)} %get-tuple-element.38), channel_id=1, source_target_pairs={{0,4},{2,6},{4,0},{6,2},{8,12},{10,14},{12,8},{14,10},{1,5},{3,7},... | collective-permute-start | bytes 4718600 | tf_op jit(solution)/shard_map/ppermute | solution.py:26
  455.3 73.4 %collective-permute-start.33 = (bf16[768,1024]{1,0:T(8,128)(2,1)}, bf16[768,1024]{1,0:T(8,128)(2,1)}, u32[]{:S(2)}, u32[]{:S(2)}) collective-permute-start(bf16[768,1024]{1,0:T(8,128)(2,1)} %get-tuple-element.37), channel_id=1, source_target_pairs={{0,2},{2,0},{4,6},{6,4},{8,10},{10,8},{12,14},{14,12},{1,3},{3,1},... | collective-permute-start | bytes 4718600 | tf_op jit(solution)/shard_map/ppermute | solution.py:26
  459.2 48.6 %collective-permute-start.31 = (bf16[192,512]{1,0:T(8,128)(2,1)}, bf16[192,512]{1,0:T(8,128)(2,1)}, u32[]{:S(2)}, u32[]{:S(2)}) collective-permute-start(bf16[192,512]{1,0:T(8,128)(2,1)} %pad_maximum_fusion.17), channel_id=1, source_target_pairs={{0,4},{2,6},{4,0},{6,2},{8,12},{10,14},{12,8},{14,10},{1,5},{3,7},... | collective-permute-start | bytes 589832 | tf_op jit(solution)/shard_map/ppermute | solution.py:26
  481.7 54.2 %collective-permute-start.37 = (bf16[16,8,128,64]{2,3,1,0:T(8,128)(2,1)}, bf16[16,8,128,64]{2,3,1,0:T(8,128)(2,1)}, u32[]{:S(2)}, u32[]{:S(2)}) collective-permute-start(bf16[16,8,128,64]{2,3,1,0:T(8,128)(2,1)} %copy.37), channel_id=1, source_target_pairs={{0,1},{1,0},{2,3},{3,2},{4,5},{5,4},{6,7},{7,6},{8,9},{9,8},{10,11... | collective-permute-start | bytes 6291464 | tf_op jit(solution)/shard_map/ppermute | solution.py:26
  508.8 16.8 %collective-permute-start.32 = (bf16[384,512]{1,0:T(8,128)(2,1)S(1)}, bf16[384,512]{1,0:T(8,128)(2,1)S(1)}, u32[]{:S(2)}, u32[]{:S(2)}) collective-permute-start(bf16[384,512]{1,0:T(8,128)(2,1)S(1)} %pad_maximum_fusion.13), channel_id=1, source_target_pairs={{0,2},{2,0},{4,6},{6,4},{8,10},{10,8},{12,14},{14,12},{1,3},{3,1},... | collective-permute-start | bytes 1179656 | tf_op jit(solution)/shard_map/ppermute | solution.py:26
  525.6 31.8 %collective-permute-start.36 = (bf16[16,8,64,128]{3,2,1,0:T(8,128)(2,1)}, bf16[16,8,64,128]{3,2,1,0:T(8,128)(2,1)}, u32[]{:S(2)}, u32[]{:S(2)}) collective-permute-start(bf16[16,8,64,128]{3,2,1,0:T(8,128)(2,1)} %get-tuple-element.42), channel_id=1, source_target_pairs={{0,1},{1,0},{2,3},{3,2},{4,5},{5,4},{6,7},{7,6},{8,9},{9,8},{10,11... | collective-permute-start | bytes 6291464 | tf_op jit(solution)/shard_map/ppermute | solution.py:26
  528.1 35.4 %collective-permute-start.39 = (bf16[256,4096]{1,0:T(8,128)(2,1)}, bf16[256,4096]{1,0:T(8,128)(2,1)}, u32[]{:S(2)}, u32[]{:S(2)}) collective-permute-start(bf16[256,4096]{1,0:T(8,128)(2,1)} %get-tuple-element.47), channel_id=1, source_target_pairs={{0,1},{1,0},{2,3},{3,2},{4,5},{5,4},{6,7},{7,6},{8,9},{9,8},{10,11... | collective-permute-start | bytes 6291464 | tf_op jit(solution)/shard_map/ppermute | solution.py:26
  528.6 39.3 %collective-permute-start.40 = (bf16[4096,256]{1,0:T(8,128)(2,1)}, bf16[4096,256]{1,0:T(8,128)(2,1)}, u32[]{:S(2)}, u32[]{:S(2)}) collective-permute-start(bf16[4096,256]{1,0:T(8,128)(2,1)} %get-tuple-element.49), channel_id=1, source_target_pairs={{0,1},{1,0},{2,3},{3,2},{4,5},{5,4},{6,7},{7,6},{8,9},{9,8},{10,11... | collective-permute-start | bytes 6291464 | tf_op jit(solution)/shard_map/ppermute | solution.py:26
  528.7 5.6 collective-permute-start.38
  (21 other events, 153.3 us)

commit v2 on v1

--- a/solution.py
+++ b/solution.py
@@ -32,7 +32,7 @@
     )
 
 
-def hid_sum(value):
+def hid_sum(value, arrived):
     devices = lax.axis_size("hid")
     place = lax.axis_index("hid")
     masks = [2**bit for bit in range(devices.bit_length() - 1)]
@@ -42,7 +42,8 @@
         kept = jnp.where(upper, high, low)
         sent = jnp.where(upper, low, high).astype(jnp.bfloat16)
         value = kept + partner(sent, "hid", mask).astype(jnp.float32)
-    value = value.astype(jnp.bfloat16)
+    nothing = jnp.minimum(jnp.abs(arrived[:1, :1].astype(jnp.float32)), 0.0)
+    value = (value + nothing).astype(jnp.bfloat16)
     for mask in reversed(masks):
         other = partner(value, "hid", mask)
         upper = (place & mask) != 0
@@ -52,26 +53,14 @@
     return value
 
 
-def pair_weights(tiles):
-    pairs = tiles.reshape((tiles.shape[0] // 2, 2) + tiles.shape[1:])
-    straight = jnp.concatenate([pairs[:, :, LEVELS:], pairs[:, :, 1:LEVELS]], axis=2)
-    cross = jnp.concatenate([pairs[:, :, :1], jnp.zeros_like(pairs[:, :, 1:LEVELS])], axis=2)
-    return straight, cross
-
-
-def input_weights(bfly_in):
-    straight, cross = pair_weights(bfly_in)
-    upper = jnp.concatenate([straight[:, 0], cross[:, 1]], axis=-1)
-    lower = jnp.concatenate([cross[:, 0], straight[:, 1]], axis=-1)
-    both = jnp.concatenate([upper, lower], axis=-2)
-    return both.reshape(both.shape[0], WIDE, PAIR_HID)
-
-
-def output_weights(bfly_out):
-    straight, cross = pair_weights(bfly_out)
-    upper = jnp.concatenate([straight[:, 0], cross[:, 0]], axis=-1)
-    lower = jnp.concatenate([cross[:, 1], straight[:, 1]], axis=-1)
-    return jnp.concatenate([upper, lower], axis=-2)
+def place_tiles(tiles_ref, weight_ref):
+    @pl.when(pl.program_id(0) == 0)
+    def _():
+        weight_ref[...] = jnp.zeros_like(weight_ref)
+
+    for half, level, source, side in tile_places():
+        start = source * PAIR_IN + side * IB
+        weight_ref[start : start + IB, half * BLK : (half + 1) * BLK] = tiles_ref[half, level]
 
 
 def order_matrix(order_ref, half):
@@ -81,10 +70,6 @@
 
 def widen(refs):
     return jnp.concatenate([ref[...] for ref in refs], axis=1)
-
-
-def level_columns(weight_ref):
-    return jnp.concatenate([weight_ref[0, source] for source in range(SOURCES)], axis=1)
 
 
 def spread(result, local_count, total_ref, remote_refs):
@@ -118,8 +103,10 @@
     sources = refs[:SOURCES]
     in_ref, out_ref, first_ref, low_in_b_ref, low_out_a_ref, order_ref = refs[SOURCES : SOURCES + 6]
     hidden_ref, slope_ref, total_ref, second_ref = refs[SOURCES + 6 : SOURCES + 10]
-    remote = refs[SOURCES + 10 :]
-    pre_act = dot(widen(sources), in_ref[0], 1, 0) + dot(first_ref[...], low_in_b_ref[...], 1, 0)
+    remote, (w_in, w_out) = refs[SOURCES + 10 : -2], refs[-2:]
+    place_tiles(in_ref, w_in)
+    place_tiles(out_ref, w_out)
+    pre_act = dot(widen(sources), w_in[...], 1, 0) + dot(first_ref[...], low_in_b_ref[...], 1, 0)
     cumulative = 0.5 * (1.0 + lax.erf(pre_act * inv_root_two))
     density = jnp.exp(-0.5 * pre_act * pre_act) * inv_root_tau
     activated = (pre_act * cumulative).astype(jnp.bfloat16)
@@ -130,7 +117,7 @@
         hidden_ref[:, columns] = dot(activated[:, columns], matrix, 1, 0).astype(jnp.bfloat16)
         slope_ref[:, columns] = dot(slope[:, columns], matrix, 1, 0).astype(jnp.bfloat16)
     hidden = hidden_ref[...]
-    spread(dot(hidden, level_columns(out_ref), 1, 0), local_count, total_ref, remote)
+    spread(dot(hidden, w_out[...], 1, 1), local_count, total_ref, remote)
     accumulate(second_ref, dot(hidden, low_out_a_ref[...], 1, 0))
 
 
@@ -140,8 +127,10 @@
         SOURCES : SOURCES + 7
     ]
     pre_grad_ref, total_ref, first_ref = refs[SOURCES + 7 : SOURCES + 10]
-    remote = refs[SOURCES + 10 :]
-    hidden_grad = dot(widen(sources), level_columns(out_ref), 1, 1) + dot(
+    remote, (w_in, w_out) = refs[SOURCES + 10 : -2], refs[-2:]
+    place_tiles(in_ref, w_in)
+    place_tiles(out_ref, w_out)
+    hidden_grad = dot(widen(sources), w_out[...], 1, 0) + dot(
         second_ref[...], low_out_a_ref[...], 1, 1
     )
     ordered = (hidden_grad * slope_ref[...].astype(jnp.float32)).astype(jnp.bfloat16)
@@ -150,7 +139,7 @@
         columns = slice(half * BLK, (half + 1) * BLK)
         pre_grad_ref[:, columns] = dot(ordered[:, columns], matrix, 1, 1).astype(jnp.bfloat16)
     pre_grad = pre_grad_ref[...]
-    spread(dot(pre_grad, in_ref[0], 1, 1), local_count, total_ref, remote)
+    spread(dot(pre_grad, w_in[...], 1, 1), local_count, total_ref, remote)
     accumulate(first_ref, dot(pre_grad, low_in_b_ref[...], 1, 1))
 
 
@@ -167,37 +156,35 @@
             yield half, level, source, half
 
 
-def grad_in_kernel(scale, *refs):
-    sources = refs[:SOURCES]
-    pre_grad_ref, first_ref, tile_keep, tile_send, low_keep, low_send = refs[SOURCES:]
-    pre_grad = pre_grad_ref[...]
-    tiles = dot(widen(sources), pre_grad, 0, 0) * scale
+def keep_tiles(scale, sources, unit_values, tile_keep, tile_send):
+    tiles = dot(widen(sources), unit_values, 0, 0) * scale
     for half, level, source, side in tile_places():
         start = source * PAIR_IN + side * IB
         tile = tiles[start : start + IB, half * BLK : (half + 1) * BLK]
         keep_and_send(
             tile[:, : BLK // 2], tile[:, BLK // 2 :], tile_keep, tile_send, (half, level)
         )
+
+
+def grad_in_kernel(scale, *refs):
+    pre_grad_ref, first_ref, tile_keep, tile_send, low_keep, low_send = refs[SOURCES:]
+    pre_grad = pre_grad_ref[...]
+    keep_tiles(scale, refs[:SOURCES], pre_grad, tile_keep, tile_send)
     low = dot(first_ref[...], pre_grad, 0, 0) * scale
     middle = low.shape[0] // 2
     keep_and_send(low[:middle], low[middle:], low_keep, low_send)
 
 
 def grad_out_kernel(scale, *refs):
-    sources = refs[:SOURCES]
     hidden_ref, second_ref, tile_keep, tile_send, low_keep, low_send = refs[SOURCES:]
     hidden = hidden_ref[...]
-    tiles = dot(hidden, widen(sources), 0, 0) * scale
-    for half, level, source, side in tile_places():
-        start = source * PAIR_IN + side * IB
-        tile = tiles[half * BLK : (half + 1) * BLK, start : start + IB]
-        keep_and_send(tile[: BLK // 2], tile[BLK // 2 :], tile_keep, tile_send, (half, level))
+    keep_tiles(scale, refs[:SOURCES], hidden, tile_keep, tile_send)
     low = dot(hidden, second_ref[...], 0, 0) * scale
     middle = low.shape[1] // 2
     keep_and_send(low[:, :middle], low[:, middle:], low_keep, low_send)
 
 
-def call(kernel, pairs, in_specs, out_specs, out_shape, args, flops):
+def call(kernel, pairs, in_specs, out_specs, out_shape, args, flops, scratch=()):
     size = sum(a.size * a.dtype.itemsize for a in args) + sum(
         s.size * s.dtype.itemsize for s in out_shape
     )
@@ -207,6 +194,7 @@
         in_specs=in_specs,
         out_specs=out_specs,
         out_shape=out_shape,
+        scratch_shapes=scratch,
         compiler_params=pltpu.CompilerParams(
             vmem_limit_bytes=VMEM_BYTES, dimension_semantics=("arbitrary",)
         ),
@@ -250,8 +238,8 @@
     unit_spec = pl.BlockSpec((rows, PAIR_HID), lambda p: (0, p))
     whole_rank = pl.BlockSpec((rows, rank), lambda p: (0, 0))
     whole_features = pl.BlockSpec((rows, features), lambda p: (0, 0))
-    in_spec = pl.BlockSpec((1, WIDE, PAIR_HID), lambda p: (p, 0, 0))
-    out_spec = pl.BlockSpec((1, SOURCES, PAIR_HID, PAIR_IN), lambda p: (p, 0, 0, 0))
+    tile_spec = pl.BlockSpec((2, LEVELS + 1, IB, BLK), lambda p: (p, 0, 0, 0))
+    weight_scratch = [pltpu.VMEM((WIDE, PAIR_HID), bf16)] * 2
     rank_columns = pl.BlockSpec((rank, PAIR_HID), lambda p: (0, p))
     rank_rows = pl.BlockSpec((PAIR_HID, rank), lambda p: (p, 0))
     order_spec = pl.BlockSpec((1, 2, BLK), lambda p: (p, 0, 0))
@@ -262,15 +250,14 @@
     def with_local(own, remote):
         return [own] * (1 + local_count) + remote
 
-    low_first = hid_sum(dot(tokens, low_in_a, 1, 0))
     token_sources = with_local(tokens, exchange([tokens] * remote_count))
-    w_in = input_weights(bfly_in)
-    w_out = output_weights(bfly_out)
+    low_first = hid_sum(dot(tokens, low_in_a, 1, 0), token_sources[-1])
+    out_tiles = jnp.swapaxes(bfly_out, 2, 3)
 
     hidden, slope, out_total, second_part, *out_remote = call(
         functools.partial(forward_kernel, local_count),
         pairs,
-        source_specs + [in_spec, out_spec, whole_rank, rank_columns, rank_rows, order_spec],
+        source_specs + [tile_spec, tile_spec, whole_rank, rank_columns, rank_rows, order_spec],
         [unit_spec, unit_spec, whole_features, whole_rank] + [feature_spec] * remote_count,
         [
             sds((rows, units), bf16),
@@ -279,48 +266,49 @@
             sds((rows, rank), f32),
         ]
         + remote_shapes,
-        token_sources + [w_in, w_out, low_first, low_in_b, low_out_a, order],
+        token_sources + [bfly_in, out_tiles, low_first, low_in_b, low_out_a, order],
         work * 2 * (WIDE + rank + BLK),
-    )
-    low_second = hid_sum(second_part)
+        weight_scratch,
+    )
+    out_arrived = exchange(out_remote)
+    low_second = hid_sum(second_part, out_arrived[-1])
     student_wide = out_total + dot(low_second, low_out_b, 1, 0)
-    for arrived in exchange(out_remote):
+    for arrived in out_arrived:
         student_wide = student_wide + arrived.astype(f32)
     student = student_wide.astype(bf16)
     residual_grad = (
         assigned[:, None].astype(f32) * (student.astype(f32) - teacher.astype(f32))
     ).astype(bf16)
-    grad_second = hid_sum(dot(residual_grad, low_out_b, 1, 1))
     grad_sources = with_local(residual_grad, exchange([residual_grad] * remote_count))
+    grad_second = hid_sum(dot(residual_grad, low_out_b, 1, 1), grad_sources[-1])
 
     pre_grad, feat_total, first_part, *feat_remote = call(
         functools.partial(backward_kernel, local_count),
         pairs,
         source_specs
-        + [in_spec, out_spec, whole_rank, rank_columns, rank_rows, order_spec, unit_spec],
+        + [tile_spec, tile_spec, whole_rank, rank_columns, rank_rows, order_spec, unit_spec],
         [unit_spec, whole_features, whole_rank] + [feature_spec] * remote_count,
         [sds((rows, units), bf16), sds((rows, features), f32), sds((rows, rank), f32)]
         + remote_shapes,
-        grad_sources + [w_in, w_out, grad_second, low_in_b, low_out_a, order, slope],
+        grad_sources + [bfly_in, out_tiles, grad_second, low_in_b, low_out_a, order, slope],
         work * 2 * (WIDE + rank + BLK // 2),
+        weight_scratch,
     )
     feat_arrived = exchange(feat_remote)
-    grad_first = hid_sum(first_part)
+    grad_first = hid_sum(first_part, feat_arrived[-1])
 
     tile_in = pl.BlockSpec((2, LEVELS + 1, IB, BLK // 2), lambda p: (p, 0, 0, 0))
     low_in = pl.BlockSpec((rank // 2, PAIR_HID), lambda p: (0, p))
-    tile_out = pl.BlockSpec((2, LEVELS + 1, BLK // 2, IB), lambda p: (p, 0, 0, 0))
     low_out = pl.BlockSpec((PAIR_HID, rank // 2), lambda p: (p, 0))
     tile_in_dims = (per_device, LEVELS + 1, IB, BLK // 2)
-    tile_out_dims = (per_device, LEVELS + 1, BLK // 2, IB)
     kept_out = call(
         functools.partial(grad_out_kernel, loss_scale),
         pairs,
         source_specs + [unit_spec, whole_rank],
-        [tile_out, tile_out, low_out, low_out],
+        [tile_in, tile_in, low_out, low_out],
         [
-            sds(tile_out_dims, f32),
-            sds(tile_out_dims, bf16),
+            sds(tile_in_dims, f32),
+            sds(tile_in_dims, bf16),
             sds((units, rank // 2), f32),
             sds((units, rank // 2), bf16),
         ],
@@ -353,7 +341,7 @@
         )
 
     grad_low_out_b = tok_halves(dot(low_second, residual_grad, 0, 0) * loss_scale, 0)
-    grad_bfly_out = tok_sum(kept_out[0], kept_out[1])
+    grad_bfly_out = jnp.swapaxes(tok_sum(kept_out[0], kept_out[1]), 2, 3)
     grad_low_out_a = tok_sum(kept_out[2], kept_out[3])
     grad_bfly_in = tok_sum(kept_in[0], kept_in[1])
     grad_low_in_b = tok_sum(kept_in[2], kept_in[3])

time: 573 us -> 635 us (1.11)
  waiting for transfers between devices: 293 us -> 431 us
  other arithmetic: 74.1 us -> 28.7 us
  local copies, waits for them, and re-layouts: 45.8 us -> 10.6 us
    ppermute x42, waiting for transfers between devices: 293 us -> 431 us  [partner(): return lax.ppermute(value, axis, pairs)]
    concatenate x4 -> x0, other arithmetic: 22.1 us -> none  [the longest x2 12.3 us: pair_weights(): jnp.concatenate([pairs[:, :, :1], jnp.zeros_like(pairs[:, :, 1:LEVELS])],...]
    unnamed x59 -> x49, local copies, waits for them, and re-layouts: 26.4 us -> 7.89 us
    add x6 -> x5, other arithmetic: 26.2 us -> 9.55 us  [tok_sum(): return keep + partner(send, 'tok', 1).astype(f32)]
  transfers between devices with their start and end apart: 42 -> 42, of which waited for: 21 -> 25; matrix products, arithmetic and copies ran while one was open for 19% -> 5% of each run, Pallas kernels for 6% -> 5%
where the time goes in v2:
time: 635 us; the launch traced here: 634 us
  waiting for transfers between devices  431 us (68%)
  Pallas kernels  107 us (17%)
  starting transfers between devices  42.9 us (7%)
  other arithmetic  28.7 us (5%)
  local copies, waits for them, and re-layouts  10.6 us (2%)
  matrix products  10.5 us (2%)
    ppermute x42, waiting for transfers between devices, partner(): return lax.ppermute(value, axis, pairs)  431 us
    pallas_call x4, Pallas kernels, call(): pl.pallas_call(kernel, grid=(pairs,), in_specs=in_specs, out_specs=out_sp...  107 us
    ppermute x42, starting transfers between devices, partner(): return lax.ppermute(value, axis, pairs)  42.9 us
  transfers between devices with their start and end apart: 42, of which 25 were waited for; matrix products, arithmetic and copies ran while one was open for 5% of the time, Pallas kernels for 5%

profile of v2, /device:TPU:0, one launch (start us, length us, event | category | flops | bytes accessed | tf_op | source)
XLA Modules:
  0.0 634.2 jit_solution(9312707988927448024)
XLA Ops:
  0.7 2.8 fusion.6
  3.5 3.0 collective-permute-start.3
  6.5 2.6 collective-permute-start.2
  9.1 6.6 %collective-permute-done.3 = bf16[384,512]{1,0:T(8,128)(2,1)} collective-permute-done((bf16[384,512]{1,0:T(8,128)(2,1)S(1)}, bf16[384,512]{1,0:T(8,128)(2,1)}, u32[]{:S(2)}, u32[]{:S(2)}) %collective-permute-start.3) | collective-permute-done | bytes 393248 | tf_op jit(solution)/shard_map/ppermute | solution.py:26
  17.0 1.9 collective-permute-start.4
  18.9 28.1 %collective-permute-done.4 = bf16[192,512]{1,0:T(8,128)(2,1)S(1)} collective-permute-done((bf16[192,512]{1,0:T(8,128)(2,1)S(1)}, bf16[192,512]{1,0:T(8,128)(2,1)S(1)}, u32[]{:S(2)}, u32[]{:S(2)}) %collective-permute-start.4) | collective-permute-done | bytes 196640 | tf_op jit(solution)/shard_map/ppermute | solution.py:26
  47.1 2.4 collective-permute-start.5
  49.5 31.0 %collective-permute-done.2.refs_6_ = bf16[768,1024]{1,0:T(8,128)(2,1)} collective-permute-done((bf16[768,1024]{1,0:T(8,128)(2,1)}, bf16[768,1024]{1,0:T(8,128)(2,1)}, u32[]{:S(2)}, u32[]{:S(2)}) %collective-permute-start.2) | collective-permute-done | bytes 1572896 | tf_op jit(solution)/shard_map/ppermute | solution.py:26
  83.0 3.1 collective-permute-start.1
  86.1 3.0 collective-permute-done.6
  89.3 36.3 %collective-permute-done.7 = bf16[192,512]{1,0:T(8,128)(2,1)S(1)} collective-permute-done((bf16[192,512]{1,0:T(8,128)(2,1)S(1)}, bf16[192,512]{1,0:T(8,128)(2,1)S(1)}, u32[]{:S(2)}, u32[]{:S(2)}) %collective-permute-start.7) | collective-permute-done | bytes 196640 | tf_op jit(solution)/shard_map/ppermute | solution.py:26
  127.2 8.8 %collective-permute-done.8 = bf16[384,512]{1,0:T(8,128)(2,1)S(1)} collective-permute-done((bf16[384,512]{1,0:T(8,128)(2,1)S(1)}, bf16[384,512]{1,0:T(8,128)(2,1)S(1)}, u32[]{:S(2)}, u32[]{:S(2)}) %collective-permute-start.8) | collective-permute-done | bytes 393248 | tf_op jit(solution)/shard_map/ppermute | solution.py:26
  136.2 39.0 %shard_map.161 = (bf16[768,4096]{1,0:T(8,128)(2,1)}, bf16[768,4096]{1,0:T(8,128)(2,1)}, f32[768,1024]{1,0:T(8,128)}, f32[768,512]{1,0:T(8,128)}, bf16[768,1024]{...) custom-call(bf16[768,1024]{1,0:T(8,128)(2,1)} %refs_3_.3, bf16[768,1024]{1,0:T(8,128)(2,1)} %refs_3_.3, ...), custom_call_target="tpu_custom_call" | custom-call | flops 20937965568 | bytes 50610176 | tf_op jit(solution)/shard_map/pallas_call | solution.py:191
  176.7 1.8 collective-permute-start.9
  179.4 6.9 %collective-permute-done.9 = bf16[384,512]{1,0:T(8,128)(2,1)S(1)} collective-permute-done((bf16[384,512]{1,0:T(8,128)(2,1)S(1)}, bf16[384,512]{1,0:T(8,128)(2,1)S(1)}, u32[]{:S(2)}, u32[]{:S(2)}) %collective-permute-start.9) | collective-permute-done | bytes 393248 | tf_op jit(solution)/shard_map/ppermute | solution.py:26
  188.2 28.4 %collective-permute-done.10 = bf16[192,512]{1,0:T(8,128)(2,1)S(1)} collective-permute-done((bf16[192,512]{1,0:T(8,128)(2,1)S(1)}, bf16[192,512]{1,0:T(8,128)(2,1)S(1)}, u32[]{:S(2)}, u32[]{:S(2)}) %collective-permute-start.10) | collective-permute-done | bytes 196640 | tf_op jit(solution)/shard_map/ppermute | solution.py:26
  216.7 3.3 collective-permute-start.11
  220.0 31.0 %collective-permute-done.12 = bf16[768,1024]{1,0:T(8,128)(2,1)S(1)} collective-permute-done((bf16[768,1024]{1,0:T(8,128)(2,1)}, bf16[768,1024]{1,0:T(8,128)(2,1)S(1)}, u32[]{:S(2)}, u32[]{:S(2)}) %collective-permute-start.12) | collective-permute-done | bytes 1572896 | tf_op jit(solution)/shard_map/ppermute | solution.py:26
  252.3 2.9 collective-permute-start.17
  255.6 3.6 collective-permute-done.13
  259.3 35.8 %collective-permute-done.14 = bf16[192,512]{1,0:T(8,128)(2,1)S(1)} collective-permute-done((bf16[192,512]{1,0:T(8,128)(2,1)S(1)}, bf16[192,512]{1,0:T(8,128)(2,1)S(1)}, u32[]{:S(2)}, u32[]{:S(2)}) %collective-permute-start.14) | collective-permute-done | bytes 196640 | tf_op jit(solution)/shard_map/ppermute | solution.py:26
  295.6 9.8 %collective-permute-done.15 = bf16[384,512]{1,0:T(8,128)(2,1)S(1)} collective-permute-done((bf16[384,512]{1,0:T(8,128)(2,1)S(1)}, bf16[384,512]{1,0:T(8,128)(2,1)S(1)}, u32[]{:S(2)}, u32[]{:S(2)}) %collective-permute-start.15) | collective-permute-done | bytes 393248 | tf_op jit(solution)/shard_map/ppermute | solution.py:26
  308.3 3.3 multiply_convert_fusion
  314.4 7.5 %collective-permute-done.21 = bf16[384,512]{1,0:T(8,128)(2,1)S(1)} collective-permute-done((bf16[384,512]{1,0:T(8,128)(2,1)S(1)}, bf16[384,512]{1,0:T(8,128)(2,1)S(1)}, u32[]{:S(2)}, u32[]{:S(2)}) %collective-permute-start.21) | collective-permute-done | bytes 393248 | tf_op jit(solution)/shard_map/ppermute | solution.py:26
  322.3 29.0 %collective-permute-done.22 = bf16[192,512]{1,0:T(8,128)(2,1)S(1)} collective-permute-done((bf16[192,512]{1,0:T(8,128)(2,1)S(1)}, bf16[192,512]{1,0:T(8,128)(2,1)S(1)}, u32[]{:S(2)}, u32[]{:S(2)}) %collective-permute-start.22) | collective-permute-done | bytes 196640 | tf_op jit(solution)/shard_map/ppermute | solution.py:26
  352.9 30.9 %collective-permute-done.20.refs_6_ = bf16[768,1024]{1,0:T(8,128)(2,1)S(1)} collective-permute-done((bf16[768,1024]{1,0:T(8,128)(2,1)S(1)}, bf16[768,1024]{1,0:T(8,128)(2,1)S(1)}, u32[]{:S(2)}, u32[]{:S(2)}) %collective-permute-start.20) | collective-permute-done | bytes 1572896 | tf_op jit(solution)/shard_map/ppermute | solution.py:26
  387.6 3.1 collective-permute-start.19
  390.8 2.6 collective-permute-done.24
  393.5 37.2 %collective-permute-done.25 = bf16[192,512]{1,0:T(8,128)(2,1)S(1)} collective-permute-done((bf16[192,512]{1,0:T(8,128)(2,1)S(1)}, bf16[192,512]{1,0:T(8,128)(2,1)S(1)}, u32[]{:S(2)}, u32[]{:S(2)}) %collective-permute-start.25) | collective-permute-done | bytes 196640 | tf_op jit(solution)/shard_map/ppermute | solution.py:26
  431.3 10.0 %collective-permute-done.26 = bf16[384,512]{1,0:T(8,128)(2,1)S(1)} collective-permute-done((bf16[384,512]{1,0:T(8,128)(2,1)S(1)}, bf16[384,512]{1,0:T(8,128)(2,1)S(1)}, u32[]{:S(2)}, u32[]{:S(2)}) %collective-permute-start.26) | collective-permute-done | bytes 393248 | tf_op jit(solution)/shard_map/ppermute | solution.py:26
  443.2 35.6 %shard_map.162 = (bf16[768,4096]{1,0:T(8,128)(2,1)}, f32[768,1024]{1,0:T(8,128)}, f32[768,512]{1,0:T(8,128)}, bf16[768,1024]{1,0:T(8,128)(2,1)}, bf16[768,1024]{1,0:T(8,128)(2,1)}, /*index=5*/bf16[768,1024]{1,0:T(8,128)(2,1)}) custom-call(bf16[768,1024]{1,0:T(8,128)(2,1)} %copy-done.10, bf16[768,1024]{1,0:T(8,128)(2,1)} %copy-done.10, ...), custom_call_target="tpu_custom_call" | custom-call | flops 19327352832 | bytes 50610176 | tf_op jit(solution)/shard_map/pallas_call | solution.py:191
  478.8 2.2 select_convert_fusion.2
  481.3 2.2 convolution_multiply_fusion
  483.6 7.2 %collective-permute-done.27 = bf16[384,512]{1,0:T(8,128)(2,1)} collective-permute-done((bf16[384,512]{1,0:T(8,128)(2,1)}, bf16[384,512]{1,0:T(8,128)(2,1)}, u32[]{:S(2)}, u32[]{:S(2)}) %collective-permute-start.27) | collective-permute-done | bytes 393248 | tf_op jit(solution)/shard_map/ppermute | solution.py:26
  492.1 16.2 %shard_map.163 = (f32[16,8,64,128]{3,2,1,0:T(8,128)}, bf16[16,8,64,128]{3,2,1,0:T(8,128)(2,1)}, f32[256,4096]{1,0:T(8,128)}, bf16[256,4096]{1,0:T(8,128)(2,1)}) custom-call(bf16[768,1024]{1,0:T(8,128)(2,1)} %refs_3_.3, bf16[768,1024]{1,0:T(8,128)(2,1)} %refs_3_.3, bf16[768,1024]{1,0:T(8,128)(2,1)} %refs_3_.3, bf16[768,1024]{1,0:T(8,128)(2,1)} %refs_3_.3, ...), custom_call_target="tpu_custom_call" | custom-call | flops 8858370048 | bytes 30670848 | tf_op jit(solution)/shard_map/pallas_call | solution.py:191
  508.4 12.0 %collective-permute-done.28 = bf16[192,512]{1,0:T(8,128)(2,1)S(1)} collective-permute-done((bf16[192,512]{1,0:T(8,128)(2,1)S(1)}, bf16[192,512]{1,0:T(8,128)(2,1)S(1)}, u32[]{:S(2)}, u32[]{:S(2)}) %collective-permute-start.28) | collective-permute-done | bytes 196640 | tf_op jit(solution)/shard_map/ppermute | solution.py:26
  520.5 2.8 collective-permute-start.29
  523.9 30.2 %collective-permute-done.30 = bf16[768,1024]{1,0:T(8,128)(2,1)S(1)} collective-permute-done((bf16[768,1024]{1,0:T(8,128)(2,1)}, bf16[768,1024]{1,0:T(8,128)(2,1)S(1)}, u32[]{:S(2)}, u32[]{:S(2)}) %collective-permute-start.30) | collective-permute-done | bytes 1572896 | tf_op jit(solution)/shard_map/ppermute | solution.py:26
  556.3 16.0 %shard_map.164 = (f32[16,8,64,128]{3,2,1,0:T(8,128)}, bf16[16,8,64,128]{3,2,1,0:T(8,128)(2,1)}, f32[4096,256]{1,0:T(8,128)}, bf16[4096,256]{1,0:T(8,128)(2,1)}) custom-call(bf16[768,1024]{1,0:T(8,128)(2,1)} %copy-done.10, bf16[768,1024]{1,0:T(8,128)(2,1)} %copy-done.10, bf16[768,1024]{1,0:T(8,128)(2,1)} %copy-done.10, bf16[768,1024]{1,0:T(8,128)(2,1)} %copy-done.10, ...), custom_call_target="tpu_custom_call" | custom-call | flops 8858370048 | bytes 30670848 | tf_op jit(solution)/shard_map/pallas_call | solution.py:191
  572.5 2.7 collective-permute-start.32
  576.5 4.4 collective-permute-done.32
  582.9 2.8 convert_add_fusion.2
  586.3 2.7 convert_add_fusion.1
  590.0 2.6 convert_add_fusion
  593.7 3.1 add_bitcast_fusion
  596.7 28.6 %collective-permute-done.33 = bf16[384,512]{1,0:T(8,128)(2,1)S(1)} collective-permute-done((bf16[384,512]{1,0:T(8,128)(2,1)S(1)}, bf16[384,512]{1,0:T(8,128)(2,1)S(1)}, u32[]{:S(2)}, u32[]{:S(2)}) %collective-permute-start.33) | collective-permute-done | bytes 393248 | tf_op jit(solution)/shard_map/ppermute | solution.py:26
  625.5 2.5 multiply_bitcast_fusion
  630.0 2.7 add_convert_fusion
  (157 shorter events, 38.1 us)
Async XLA Ops:
  0.6 305.0 %copy-start = (bf16[512,1024]{1,0:T(8,128)(2,1)S(1)}, bf16[512,1024]{1,0:T(8,128)(2,1)}, u32[]{:S(2)}) copy-start(bf16[512,1024]{1,0:T(8,128)(2,1)} %param.18) | copy-start | bytes 3145732
  3.5 12.2 %collective-permute-start.3 = (bf16[384,512]{1,0:T(8,128)(2,1)S(1)}, bf16[384,512]{1,0:T(8,128)(2,1)}, u32[]{:S(2)}, u32[]{:S(2)}) collective-permute-start(bf16[384,512]{1,0:T(8,128)(2,1)S(1)} %select_convert_fusion.5), channel_id=1, source_target_pairs={{0,2},{2,0},{4,6},{6,4},{8,10},{10,8},{12,14},{14,12},{1,3},{3,1},... | collective-permute-start | bytes 1179656 | tf_op jit(solution)/shard_map/ppermute | solution.py:26
  6.5 73.9 %collective-permute-start.2 = (bf16[768,1024]{1,0:T(8,128)(2,1)}, bf16[768,1024]{1,0:T(8,128)(2,1)}, u32[]{:S(2)}, u32[]{:S(2)}) collective-permute-start(bf16[768,1024]{1,0:T(8,128)(2,1)} %refs_3_.3), channel_id=1, source_target_pairs={{0,8},{2,10},{4,12},{6,14},{8,0},{10,2},{12,4},{14,6},{1,9},{3,11}... | collective-permute-start | bytes 4718600 | tf_op jit(solution)/shard_map/ppermute | solution.py:26
  17.0 30.0 %collective-permute-start.4 = (bf16[192,512]{1,0:T(8,128)(2,1)S(1)}, bf16[192,512]{1,0:T(8,128)(2,1)S(1)}, u32[]{:S(2)}, u32[]{:S(2)}) collective-permute-start(bf16[192,512]{1,0:T(8,128)(2,1)S(1)} %select_convert_fusion.9), channel_id=1, source_target_pairs={{0,4},{2,6},{4,0},{6,2},{8,12},{10,14},{12,8},{14,10},{1,5},{3,7},... | collective-permute-start | bytes 589832 | tf_op jit(solution)/shard_map/ppermute | solution.py:26
  18.9 108.3 %copy-start.15 = (s32[16,256]{1,0:T(8,128)S(1)}, s32[16,256]{1,0:T(8,128)}, u32[]{:S(2)}) copy-start(s32[16,256]{1,0:T(8,128)} %param.19) | copy-start | bytes 49156
  47.1 35.2 %collective-permute-start.5 = (bf16[96,512]{1,0:T(8,128)(2,1)S(1)}, bf16[96,512]{1,0:T(8,128)(2,1)S(1)}, u32[]{:S(2)}, u32[]{:S(2)}) collective-permute-start(bf16[96,512]{1,0:T(8,128)(2,1)S(1)} %select_convert_fusion.13), channel_id=1, source_target_pairs={{0,8},{2,10},{4,12},{6,14},{8,0},{10,2},{12,4},{14,6},{1,9},{3,11}... | collective-permute-start | bytes 294920 | tf_op jit(solution)/shard_map/ppermute | solution.py:26
  82.3 6.8 %collective-permute-start.6 = (bf16[96,512]{1,0:T(8,128)(2,1)S(1)}, bf16[96,512]{1,0:T(8,128)(2,1)S(1)}, u32[]{:S(2)}, u32[]{:S(2)}) collective-permute-start(bf16[96,512]{1,0:T(8,128)(2,1)S(1)} %add_convert_fusion.5), channel_id=1, source_target_pairs={{0,8},{2,10},{4,12},{6,14},{8,0},{10,2},{12,4},{14,6},{1,9},{3,11}... | collective-permute-start | bytes 294920 | tf_op jit(solution)/shard_map/ppermute | solution.py:26
  82.4 53.7 %collective-permute-start = (bf16[768,1024]{1,0:T(8,128)(2,1)}, bf16[768,1024]{1,0:T(8,128)(2,1)}, u32[]{:S(2)}, u32[]{:S(2)}) collective-permute-start(bf16[768,1024]{1,0:T(8,128)(2,1)} %refs_3_.3), channel_id=1, source_target_pairs={{0,2},{2,0},{4,6},{6,4},{8,10},{10,8},{12,14},{14,12},{1,3},{3,1},... | collective-permute-start | bytes 4718600 | tf_op jit(solution)/shard_map/ppermute | solution.py:26
  83.0 53.2 %collective-permute-start.1 = (bf16[768,1024]{1,0:T(8,128)(2,1)}, bf16[768,1024]{1,0:T(8,128)(2,1)}, u32[]{:S(2)}, u32[]{:S(2)}) collective-permute-start(bf16[768,1024]{1,0:T(8,128)(2,1)} %refs_3_.3), channel_id=1, source_target_pairs={{0,4},{2,6},{4,0},{6,2},{8,12},{10,14},{12,8},{14,10},{1,5},{3,7},... | collective-permute-start | bytes 4718600 | tf_op jit(solution)/shard_map/ppermute | solution.py:26
  89.2 36.4 %collective-permute-start.7 = (bf16[192,512]{1,0:T(8,128)(2,1)S(1)}, bf16[192,512]{1,0:T(8,128)(2,1)S(1)}, u32[]{:S(2)}, u32[]{:S(2)}) collective-permute-start(bf16[192,512]{1,0:T(8,128)(2,1)S(1)} %pad_maximum_fusion.12), channel_id=1, source_target_pairs={{0,4},{2,6},{4,0},{6,2},{8,12},{10,14},{12,8},{14,10},{1,5},{3,7},... | collective-permute-start | bytes 589832 | tf_op jit(solution)/shard_map/ppermute | solution.py:26
  125.7 10.2 %collective-permute-start.8 = (bf16[384,512]{1,0:T(8,128)(2,1)S(1)}, bf16[384,512]{1,0:T(8,128)(2,1)S(1)}, u32[]{:S(2)}, u32[]{:S(2)}) collective-permute-start(bf16[384,512]{1,0:T(8,128)(2,1)S(1)} %pad_maximum_fusion.8), channel_id=1, source_target_pairs={{0,2},{2,0},{4,6},{6,4},{8,10},{10,8},{12,14},{14,12},{1,3},{3,1},... | collective-permute-start | bytes 1179656 | tf_op jit(solution)/shard_map/ppermute | solution.py:26
  176.7 9.7 %collective-permute-start.9 = (bf16[384,512]{1,0:T(8,128)(2,1)S(1)}, bf16[384,512]{1,0:T(8,128)(2,1)S(1)}, u32[]{:S(2)}, u32[]{:S(2)}) collective-permute-start(bf16[384,512]{1,0:T(8,128)(2,1)S(1)} %select_convert_fusion.4), channel_id=1, source_target_pairs={{0,2},{2,0},{4,6},{6,4},{8,10},{10,8},{12,14},{14,12},{1,3},{3,1},... | collective-permute-start | bytes 1179656 | tf_op jit(solution)/shard_map/ppermute | solution.py:26
  178.5 72.5 %collective-permute-start.12 = (bf16[768,1024]{1,0:T(8,128)(2,1)}, bf16[768,1024]{1,0:T(8,128)(2,1)S(1)}, u32[]{:S(2)}, u32[]{:S(2)}) collective-permute-start(bf16[768,1024]{1,0:T(8,128)(2,1)} %get-tuple-element.31), channel_id=1, source_target_pairs={{0,8},{2,10},{4,12},{6,14},{8,0},{10,2},{12,4},{14,6},{1,9},{3,11}... | collective-permute-start | bytes 4718600 | tf_op jit(solution)/shard_map/ppermute | solution.py:26
  186.4 65.9 %copy-start.23 = (bf16[768,1024]{1,0:T(8,128)(2,1)S(1)}, bf16[768,1024]{1,0:T(8,128)(2,1)}, u32[]{:S(2)}) copy-start(bf16[768,1024]{1,0:T(8,128)(2,1)} %get-tuple-element.33) | copy-start | bytes 4718596
  188.1 67.1 %copy-start.22 = (bf16[768,1024]{1,0:T(8,128)(2,1)S(1)}, bf16[768,1024]{1,0:T(8,128)(2,1)}, u32[]{:S(2)}) copy-start(bf16[768,1024]{1,0:T(8,128)(2,1)} %get-tuple-element.32) | copy-start | bytes 4718596
  188.1 107.5 %copy-start.16 = (s32[768]{0:T(1024)S(1)}, s32[768]{0:T(1024)}, u32[]{:S(2)}) copy-start(s32[768]{0:T(1024)} %param.12) | copy-start | bytes 9220
  188.1 28.4 %collective-permute-start.10 = (bf16[192,512]{1,0:T(8,128)(2,1)S(1)}, bf16[192,512]{1,0:T(8,128)(2,1)S(1)}, u32[]{:S(2)}, u32[]{:S(2)}) collective-permute-start(bf16[192,512]{1,0:T(8,128)(2,1)S(1)} %select_convert_fusion.8), channel_id=1, source_target_pairs={{0,4},{2,6},{4,0},{6,2},{8,12},{10,14},{12,8},{14,10},{1,5},{3,7},... | collective-permute-start | bytes 589832 | tf_op jit(solution)/shard_map/ppermute | solution.py:26
  216.7 35.4 %collective-permute-start.11 = (bf16[96,512]{1,0:T(8,128)(2,1)S(1)}, bf16[96,512]{1,0:T(8,128)(2,1)S(1)}, u32[]{:S(2)}, u32[]{:S(2)}) collective-permute-start(bf16[96,512]{1,0:T(8,128)(2,1)S(1)} %select_convert_fusion.12), channel_id=1, source_target_pairs={{0,8},{2,10},{4,12},{6,14},{8,0},{10,2},{12,4},{14,6},{1,9},{3,11}... | collective-permute-start | bytes 294920 | tf_op jit(solution)/shard_map/ppermute | solution.py:26
  252.2 7.0 %collective-permute-start.13 = (bf16[96,512]{1,0:T(8,128)(2,1)S(1)}, bf16[96,512]{1,0:T(8,128)(2,1)S(1)}, u32[]{:S(2)}, u32[]{:S(2)}) collective-permute-start(bf16[96,512]{1,0:T(8,128)(2,1)S(1)} %add_convert_fusion.4), channel_id=1, source_target_pairs={{0,8},{2,10},{4,12},{6,14},{8,0},{10,2},{12,4},{14,6},{1,9},{3,11}... | collective-permute-start | bytes 294920 | tf_op jit(solution)/shard_map/ppermute | solution.py:26
  252.3 54.4 %collective-permute-start.17 = (bf16[768,1024]{1,0:T(8,128)(2,1)S(1)}, bf16[768,1024]{1,0:T(8,128)(2,1)S(1)}, u32[]{:S(2)}, u32[]{:S(2)}) collective-permute-start(bf16[768,1024]{1,0:T(8,128)(2,1)S(1)} %copy-done.23), channel_id=1, source_target_pairs={{0,4},{2,6},{4,0},{6,2},{8,12},{10,14},{12,8},{14,10},{1,5},{3,7},... | collective-permute-start | bytes 4718600 | tf_op jit(solution)/shard_map/ppermute | solution.py:26
  255.2 51.5 %collective-permute-start.16 = (bf16[768,1024]{1,0:T(8,128)(2,1)S(1)}, bf16[768,1024]{1,0:T(8,128)(2,1)S(1)}, u32[]{:S(2)}, u32[]{:S(2)}) collective-permute-start(bf16[768,1024]{1,0:T(8,128)(2,1)S(1)} %copy-done.22), channel_id=1, source_target_pairs={{0,2},{2,0},{4,6},{6,4},{8,10},{10,8},{12,14},{14,12},{1,3},{3,1},... | collective-permute-start | bytes 4718600 | tf_op jit(solution)/shard_map/ppermute | solution.py:26
  259.2 35.8 %collective-permute-start.14 = (bf16[192,512]{1,0:T(8,128)(2,1)S(1)}, bf16[192,512]{1,0:T(8,128)(2,1)S(1)}, u32[]{:S(2)}, u32[]{:S(2)}) collective-permute-start(bf16[192,512]{1,0:T(8,128)(2,1)S(1)} %pad_maximum_fusion.13), channel_id=1, source_target_pairs={{0,4},{2,6},{4,0},{6,2},{8,12},{10,14},{12,8},{14,10},{1,5},{3,7},... | collective-permute-start | bytes 589832 | tf_op jit(solution)/shard_map/ppermute | solution.py:26
  295.2 10.3 %collective-permute-start.15 = (bf16[384,512]{1,0:T(8,128)(2,1)S(1)}, bf16[384,512]{1,0:T(8,128)(2,1)S(1)}, u32[]{:S(2)}, u32[]{:S(2)}) collective-permute-start(bf16[384,512]{1,0:T(8,128)(2,1)S(1)} %pad_maximum_fusion.9), channel_id=1, source_target_pairs={{0,2},{2,0},{4,6},{6,4},{8,10},{10,8},{12,14},{14,12},{1,3},{3,1},... | collective-permute-start | bytes 1179656 | tf_op jit(solution)/shard_map/ppermute | solution.py:26
  311.5 76.1 %copy-start.10 = (bf16[768,1024]{1,0:T(8,128)(2,1)}, bf16[768,1024]{1,0:T(8,128)(2,1)S(1)}, u32[]{:S(2)}) copy-start(bf16[768,1024]{1,0:T(8,128)(2,1)S(1)} %get-tuple-element.58.refs_0_.refs_1_.refs_2_.refs_3_) | copy-start | bytes 4718596
  312.6 9.3 %collective-permute-start.21 = (bf16[384,512]{1,0:T(8,128)(2,1)S(1)}, bf16[384,512]{1,0:T(8,128)(2,1)S(1)}, u32[]{:S(2)}, u32[]{:S(2)}) collective-permute-start(bf16[384,512]{1,0:T(8,128)(2,1)S(1)} %select_convert_fusion.3), channel_id=1, source_target_pairs={{0,2},{2,0},{4,6},{6,4},{8,10},{10,8},{12,14},{14,12},{1,3},{3,1},... | collective-permute-start | bytes 1179656 | tf_op jit(solution)/shard_map/ppermute | solution.py:26
  313.0 70.7 %collective-permute-start.20 = (bf16[768,1024]{1,0:T(8,128)(2,1)S(1)}, bf16[768,1024]{1,0:T(8,128)(2,1)S(1)}, u32[]{:S(2)}, u32[]{:S(2)}) collective-permute-start(bf16[768,1024]{1,0:T(8,128)(2,1)S(1)} %get-tuple-element.58.refs_0_.refs_1_.refs_2_.refs_3_), channel_id=1, source_target_pairs={{0,8},{2,10},{4,12},{6,14},{8,0},{10,2},{12,4},{14,6},{1,9},{3,11}... | collective-permute-start | bytes 4718600 | tf_op jit(solution)/shard_map/ppermute | solution.py:26
  322.2 29.0 %collective-permute-start.22 = (bf16[192,512]{1,0:T(8,128)(2,1)S(1)}, bf16[192,512]{1,0:T(8,128)(2,1)S(1)}, u32[]{:S(2)}, u32[]{:S(2)}) collective-permute-start(bf16[192,512]{1,0:T(8,128)(2,1)S(1)} %select_convert_fusion.7), channel_id=1, source_target_pairs={{0,4},{2,6},{4,0},{6,2},{8,12},{10,14},{12,8},{14,10},{1,5},{3,7},... | collective-permute-start | bytes 589832 | tf_op jit(solution)/shard_map/ppermute | solution.py:26
  351.4 34.4 %collective-permute-start.23 = (bf16[96,512]{1,0:T(8,128)(2,1)S(1)}, bf16[96,512]{1,0:T(8,128)(2,1)S(1)}, u32[]{:S(2)}, u32[]{:S(2)}) collective-permute-start(bf16[96,512]{1,0:T(8,128)(2,1)S(1)} %select_convert_fusion.11), channel_id=1, source_target_pairs={{0,8},{2,10},{4,12},{6,14},{8,0},{10,2},{12,4},{14,6},{1,9},{3,11}... | collective-permute-start | bytes 294920 | tf_op jit(solution)/shard_map/ppermute | solution.py:26
  385.8 7.5 %collective-permute-start.24 = (bf16[96,512]{1,0:T(8,128)(2,1)S(1)}, bf16[96,512]{1,0:T(8,128)(2,1)S(1)}, u32[]{:S(2)}, u32[]{:S(2)}) collective-permute-start(bf16[96,512]{1,0:T(8,128)(2,1)S(1)} %add_convert_fusion.3), channel_id=1, source_target_pairs={{0,8},{2,10},{4,12},{6,14},{8,0},{10,2},{12,4},{14,6},{1,9},{3,11}... | collective-permute-start | bytes 294920 | tf_op jit(solution)/shard_map/ppermute | solution.py:26
  385.9 55.5 %collective-permute-start.18 = (bf16[768,1024]{1,0:T(8,128)(2,1)S(1)}, bf16[768,1024]{1,0:T(8,128)(2,1)S(1)}, u32[]{:S(2)}, u32[]{:S(2)}) collective-permute-start(bf16[768,1024]{1,0:T(8,128)(2,1)S(1)} %get-tuple-element.58.refs_0_.refs_1_.refs_2_.refs_3_), channel_id=1, source_target_pairs={{0,2},{2,0},{4,6},{6,4},{8,10},{10,8},{12,14},{14,12},{1,3},{3,1},... | collective-permute-start | bytes 4718600 | tf_op jit(solution)/shard_map/ppermute | solution.py:26
  387.6 53.8 %collective-permute-start.19 = (bf16[768,1024]{1,0:T(8,128)(2,1)S(1)}, bf16[768,1024]{1,0:T(8,128)(2,1)S(1)}, u32[]{:S(2)}, u32[]{:S(2)}) collective-permute-start(bf16[768,1024]{1,0:T(8,128)(2,1)S(1)} %get-tuple-element.58.refs_0_.refs_1_.refs_2_.refs_3_), channel_id=1, source_target_pairs={{0,4},{2,6},{4,0},{6,2},{8,12},{10,14},{12,8},{14,10},{1,5},{3,7},... | collective-permute-start | bytes 4718600 | tf_op jit(solution)/shard_map/ppermute | solution.py:26
  393.4 37.2 %collective-permute-start.25 = (bf16[192,512]{1,0:T(8,128)(2,1)S(1)}, bf16[192,512]{1,0:T(8,128)(2,1)S(1)}, u32[]{:S(2)}, u32[]{:S(2)}) collective-permute-start(bf16[192,512]{1,0:T(8,128)(2,1)S(1)} %pad_maximum_fusion.14), channel_id=1, source_target_pairs={{0,4},{2,6},{4,0},{6,2},{8,12},{10,14},{12,8},{14,10},{1,5},{3,7},... | collective-permute-start | bytes 589832 | tf_op jit(solution)/shard_map/ppermute | solution.py:26
  430.7 10.5 %collective-permute-start.26 = (bf16[384,512]{1,0:T(8,128)(2,1)S(1)}, bf16[384,512]{1,0:T(8,128)(2,1)S(1)}, u32[]{:S(2)}, u32[]{:S(2)}) collective-permute-start(bf16[384,512]{1,0:T(8,128)(2,1)S(1)} %pad_maximum_fusion.10), channel_id=1, source_target_pairs={{0,2},{2,0},{4,6},{6,4},{8,10},{10,8},{12,14},{14,12},{1,3},{3,1},... | collective-permute-start | bytes 1179656 | tf_op jit(solution)/shard_map/ppermute | solution.py:26
  481.0 9.8 %collective-permute-start.27 = (bf16[384,512]{1,0:T(8,128)(2,1)}, bf16[384,512]{1,0:T(8,128)(2,1)}, u32[]{:S(2)}, u32[]{:S(2)}) collective-permute-start(bf16[384,512]{1,0:T(8,128)(2,1)} %select_convert_fusion.2), channel_id=1, source_target_pairs={{0,2},{2,0},{4,6},{6,4},{8,10},{10,8},{12,14},{14,12},{1,3},{3,1},... | collective-permute-start | bytes 1179656 | tf_op jit(solution)/shard_map/ppermute | solution.py:26
  483.5 70.6 %collective-permute-start.30 = (bf16[768,1024]{1,0:T(8,128)(2,1)}, bf16[768,1024]{1,0:T(8,128)(2,1)S(1)}, u32[]{:S(2)}, u32[]{:S(2)}) collective-permute-start(bf16[768,1024]{1,0:T(8,128)(2,1)} %get-tuple-element.37), channel_id=1, source_target_pairs={{0,8},{2,10},{4,12},{6,14},{8,0},{10,2},{12,4},{14,6},{1,9},{3,11}... | collective-permute-start | bytes 4718600 | tf_op jit(solution)/shard_map/ppermute | solution.py:26
  492.1 28.3 %collective-permute-start.28 = (bf16[192,512]{1,0:T(8,128)(2,1)S(1)}, bf16[192,512]{1,0:T(8,128)(2,1)S(1)}, u32[]{:S(2)}, u32[]{:S(2)}) collective-permute-start(bf16[192,512]{1,0:T(8,128)(2,1)S(1)} %select_convert_fusion.6), channel_id=1, source_target_pairs={{0,4},{2,6},{4,0},{6,2},{8,12},{10,14},{12,8},{14,10},{1,5},{3,7},... | collective-permute-start | bytes 589832 | tf_op jit(solution)/shard_map/ppermute | solution.py:26
  508.3 74.5 %collective-permute-start.36 = (bf16[16,8,64,128]{3,2,1,0:T(8,128)(2,1)}, bf16[16,8,64,128]{3,2,1,0:T(8,128)(2,1)S(1)}, u32[]{:S(2)}, u32[]{:S(2)}) collective-permute-start(bf16[16,8,64,128]{3,2,1,0:T(8,128)(2,1)} %get-tuple-element.42), channel_id=1, source_target_pairs={{0,1},{1,0},{2,3},{3,2},{4,5},{5,4},{6,7},{7,6},{8,9},{9,8},{10,11... | collective-permute-start | bytes 6291464 | tf_op jit(solution)/shard_map/ppermute | solution.py:26
  520.5 35.7 %collective-permute-start.29 = (bf16[96,512]{1,0:T(8,128)(2,1)S(1)}, bf16[96,512]{1,0:T(8,128)(2,1)S(1)}, u32[]{:S(2)}, u32[]{:S(2)}) collective-permute-start(bf16[96,512]{1,0:T(8,128)(2,1)S(1)} %select_convert_fusion.10), channel_id=1, source_target_pairs={{0,8},{2,10},{4,12},{6,14},{8,0},{10,2},{12,4},{14,6},{1,9},{3,11}... | collective-permute-start | bytes 294920 | tf_op jit(solution)/shard_map/ppermute | solution.py:26
  523.4 51.9 %collective-permute-start.41 = (bf16[256,1024]{1,0:T(8,128)(2,1)S(1)}, bf16[256,1024]{1,0:T(8,128)(2,1)S(1)}, u32[]{:S(2)}, u32[]{:S(2)}) collective-permute-start(bf16[256,1024]{1,0:T(8,128)(2,1)S(1)} %select_convert_fusion), channel_id=1, source_target_pairs={{0,1},{1,0},{2,3},{3,2},{4,5},{5,4},{6,7},{7,6},{8,9},{9,8},{10,11... | collective-permute-start | bytes 1572872 | tf_op jit(solution)/shard_map/ppermute | solution.py:26
  523.4 62.3 %collective-permute-start.39 = (bf16[256,4096]{1,0:T(8,128)(2,1)S(1)}, bf16[256,4096]{1,0:T(8,128)(2,1)S(1)}, u32[]{:S(2)}, u32[]{:S(2)}) collective-permute-start(bf16[256,4096]{1,0:T(8,128)(2,1)S(1)} %copy-done.17), channel_id=1, source_target_pairs={{0,1},{1,0},{2,3},{3,2},{4,5},{5,4},{6,7},{7,6},{8,9},{9,8},{10,11... | collective-permute-start | bytes 6291464 | tf_op jit(solution)/shard_map/ppermute | solution.py:26
  556.2 16.2 %collective-permute-start.31 = (bf16[96,512]{1,0:T(8,128)(2,1)S(1)}, bf16[96,512]{1,0:T(8,128)(2,1)S(1)}, u32[]{:S(2)}, u32[]{:S(2)}) collective-permute-start(bf16[96,512]{1,0:T(8,128)(2,1)S(1)} %add_convert_fusion.2), channel_id=1, source_target_pairs={{0,8},{2,10},{4,12},{6,14},{8,0},{10,2},{12,4},{14,6},{1,9},{3,11}... | collective-permute-start | bytes 294920 | tf_op jit(solution)/shard_map/ppermute | solution.py:26
  572.3 16.6 %collective-permute-start.40 = (bf16[4096,256]{1,0:T(8,128)(2,1)}, bf16[4096,256]{1,0:T(8,128)(2,1)S(1)}, u32[]{:S(2)}, u32[]{:S(2)}) collective-permute-start(bf16[4096,256]{1,0:T(8,128)(2,1)} %get-tuple-element.49), channel_id=1, source_target_pairs={{0,1},{1,0},{2,3},{3,2},{4,5},{5,4},{6,7},{7,6},{8,9},{9,8},{10,11... | collective-permute-start | bytes 6291464 | tf_op jit(solution)/shard_map/ppermute | solution.py:26
  572.5 8.5 %collective-permute-start.32 = (bf16[192,512]{1,0:T(8,128)(2,1)S(1)}, bf16[192,512]{1,0:T(8,128)(2,1)S(1)}, u32[]{:S(2)}, u32[]{:S(2)}) collective-permute-start(bf16[192,512]{1,0:T(8,128)(2,1)S(1)} %pad_maximum_fusion.15), channel_id=1, source_target_pairs={{0,4},{2,6},{4,0},{6,2},{8,12},{10,14},{12,8},{14,10},{1,5},{3,7},... | collective-permute-start | bytes 589832 | tf_op jit(solution)/shard_map/ppermute | solution.py:26
  576.5 52.8 %collective-permute-start.35 = (bf16[768,1024]{1,0:T(8,128)(2,1)}, bf16[768,1024]{1,0:T(8,128)(2,1)S(1)}, u32[]{:S(2)}, u32[]{:S(2)}) collective-permute-start(bf16[768,1024]{1,0:T(8,128)(2,1)} %get-tuple-element.39), channel_id=1, source_target_pairs={{0,4},{2,6},{4,0},{6,2},{8,12},{10,14},{12,8},{14,10},{1,5},{3,7},... | collective-permute-start | bytes 4718600 | tf_op jit(solution)/shard_map/ppermute | solution.py:26
  581.0 48.3 %collective-permute-start.34 = (bf16[768,1024]{1,0:T(8,128)(2,1)S(1)}, bf16[768,1024]{1,0:T(8,128)(2,1)S(1)}, u32[]{:S(2)}, u32[]{:S(2)}) collective-permute-start(bf16[768,1024]{1,0:T(8,128)(2,1)S(1)} %copy-done.18), channel_id=1, source_target_pairs={{0,2},{2,0},{4,6},{6,4},{8,10},{10,8},{12,14},{14,12},{1,3},{3,1},... | collective-permute-start | bytes 4718600 | tf_op jit(solution)/shard_map/ppermute | solution.py:26
  582.8 9.7 %collective-permute-start.37 = (bf16[16,8,64,128]{3,2,1,0:T(8,128)(2,1)}, bf16[16,8,64,128]{3,2,1,0:T(8,128)(2,1)S(1)}, u32[]{:S(2)}, u32[]{:S(2)}) collective-permute-start(bf16[16,8,64,128]{3,2,1,0:T(8,128)(2,1)} %get-tuple-element.45), channel_id=1, source_target_pairs={{0,1},{1,0},{2,3},{3,2},{4,5},{5,4},{6,7},{7,6},{8,9},{9,8},{10,11... | collective-permute-start | bytes 6291464 | tf_op jit(solution)/shard_map/ppermute | solution.py:26
  585.7 39.7 %collective-permute-start.33 = (bf16[384,512]{1,0:T(8,128)(2,1)S(1)}, bf16[384,512]{1,0:T(8,128)(2,1)S(1)}, u32[]{:S(2)}, u32[]{:S(2)}) collective-permute-start(bf16[384,512]{1,0:T(8,128)(2,1)S(1)} %pad_maximum_fusion.11), channel_id=1, source_target_pairs={{0,2},{2,0},{4,6},{6,4},{8,10},{10,8},{12,14},{14,12},{1,3},{3,1},... | collective-permute-start | bytes 1179656 | tf_op jit(solution)/shard_map/ppermute | solution.py:26
  628.1 4.5 collective-permute-start.38
  (18 other events, 168.7 us)
